TPU v7x, 128 devices: a whole 4x4x4 slice. The times are simulated.
128 devices in a mesh: shot: 4 (over x), blk: 32 (over z, y, core).
Axes of the slice: x: 4, y: 4, z: 4, core: 2. Of those that a mesh axis runs over, the one named last changes fastest.
Arguments:
- intensities: bfloat16 [8192, 16, 128], P('blk', 'shot'), may hold values from -6 to 6
- tile_owner: int32 [8192], P('blk'), may hold values from 0 to 31, as said below
- tile_place: int32 [8192], P('blk'), may hold values from 0 to 255
- tile_kernel: int32 [8192], P('blk'), may hold values from 0 to 3
- mask_len: int32 [8192], P('blk'), may hold values from 1 to 128
- interp_weights: bfloat16 [4, 128, 128], replicated, may hold values from 0 to 1.2
Outputs:
- corr_diff: float32 [16, 512, 2048], P('shot', 'blk')
Inputs may be any that keep to these rules, and one draw needn't show every extreme that they name: `tile_owner`: in each device's block of 256 tiles no owner is named by more than 24 tiles, and one owner, the same for every block, is named by exactly 24 tiles of every block.
All inputs are finite; a program needn't handle non-finite values.
Results may differ from a plain program's by a relative error of at most 0.0003.
Values may be sent and summed in bfloat16 or wider, within the bound.
A program may use at most 64 MiB of HBM per device.

v0:
```python
import math

import jax
import jax.numpy as jnp
from jax import lax
from jax.sharding import PartitionSpec as P

ANG = 2048
TP = 128
Q_DEV = 16
NSEG = 16


def from_behind(block, axis, distance):
    devices = range(lax.axis_size(axis))
    route = [((i - distance) % len(devices), i) for i in devices]
    return lax.ppermute(block, axis, route)


def phase_table(rows, columns, period, sign):
    row_index = lax.broadcasted_iota(jnp.int32, (rows, columns), 0)
    column_index = lax.broadcasted_iota(jnp.int32, (rows, columns), 1)
    phase_angle = (row_index * column_index % period).astype(jnp.float32) * (2.0 * math.pi / period)
    return (jnp.cos(phase_angle), sign * jnp.sin(phase_angle))


def contract(form, first_array, second_array):
    return jnp.einsum(
        form,
        first_array,
        second_array,
        precision=lax.Precision.HIGHEST,
        preferred_element_type=jnp.float32,
    )


def transform(real_in, imag_in, sign):
    row_count, length = real_in.shape
    inner = math.gcd(length, 128)
    outer = length // inner
    first_cos, first_sin = phase_table(outer, outer, outer, sign)
    twist_cos, twist_sin = phase_table(outer, inner, length, sign)
    last_cos, last_sin = phase_table(inner, inner, inner, sign)
    real_grid = real_in.reshape(row_count, outer, inner)
    section_real = contract("rab,ak->rkb", real_grid, first_cos)
    section_imag = contract("rab,ak->rkb", real_grid, first_sin)
    if imag_in is not None:
        imag_grid = imag_in.reshape(row_count, outer, inner)
        section_real = section_real - contract("rab,ak->rkb", imag_grid, first_sin)
        section_imag = section_imag + contract("rab,ak->rkb", imag_grid, first_cos)
    turned_real = section_real * twist_cos[None] - section_imag * twist_sin[None]
    turned_imag = section_real * twist_sin[None] + section_imag * twist_cos[None]
    final_real = contract("rkb,bm->rkm", turned_real, last_cos) - contract(
        "rkb,bm->rkm", turned_imag, last_sin
    )
    final_imag = contract("rkb,bm->rkm", turned_real, last_sin) + contract(
        "rkb,bm->rkm", turned_imag, last_cos
    )
    final_real = final_real.transpose(0, 2, 1).reshape(row_count, length)
    final_imag = final_imag.transpose(0, 2, 1).reshape(row_count, length)
    return (final_real, final_imag)


def interpolate(pixels, kernels, lengths, weights):
    tiles_here = pixels.shape[0]
    shot_count = pixels.shape[1]
    kernel_count = weights.shape[0]
    block_size = math.gcd(tiles_here, 256)
    block_count = tiles_here // block_size

    def one_block(block_data):
        block_pixels, block_kernels, block_lengths = block_data
        active_rows = lax.broadcasted_iota(jnp.int32, (block_size, TP), 1) < block_lengths[:, None]
        masked_intensity = jnp.where(
            active_rows[:, None, :], block_pixels, jnp.zeros_like(block_pixels)
        )
        kernel_pick = (
            block_kernels[:, None] == lax.broadcasted_iota(jnp.int32, (block_size, kernel_count), 1)
        ).astype(jnp.float32)
        all_values = jnp.einsum(
            "jsp,kpa->jksa", masked_intensity, weights, preferred_element_type=jnp.float32
        )
        all_masks = jnp.einsum(
            "jp,kpa->jka",
            active_rows.astype(jnp.bfloat16),
            weights,
            preferred_element_type=jnp.float32,
        )
        value_entries = jnp.sum(all_values * kernel_pick[:, :, None, None], axis=1)
        mask_values = jnp.sum(all_masks * kernel_pick[:, :, None], axis=1)
        return (value_entries, mask_values)

    value_entries, mask_values = lax.map(
        one_block,
        (
            pixels.reshape(block_count, block_size, shot_count, TP),
            kernels.reshape(block_count, block_size),
            lengths.reshape(block_count, block_size),
        ),
    )
    return (value_entries.reshape(tiles_here, shot_count, TP), mask_values.reshape(tiles_here, TP))


def slot_positions(owners, owner_count, capacity):
    onehot_table = (
        owners[:, None] == lax.broadcasted_iota(jnp.int32, (owners.shape[0], owner_count), 1)
    ).astype(jnp.int32)
    earlier = jnp.cumsum(onehot_table, axis=0) - onehot_table
    return owners * capacity + jnp.sum(earlier * onehot_table, axis=1)


def collect_slots(values, masks, places, slot_count):
    row_count = values.shape[0]
    shot_count = values.shape[1]
    selector = (
        places[None, :] == lax.broadcasted_iota(jnp.int32, (slot_count, row_count), 0)
    ).astype(jnp.float32)
    summed_values = jnp.dot(
        selector,
        values.reshape(row_count, shot_count * TP),
        precision=lax.Precision.HIGHEST,
        preferred_element_type=jnp.float32,
    )
    summed_masks = jnp.dot(
        selector, masks, precision=lax.Precision.HIGHEST, preferred_element_type=jnp.float32
    )
    return (summed_values.reshape(slot_count, shot_count, TP), summed_masks)


def per_device(intensities, tile_owner, tile_place, tile_kernel, mask_len, interp_weights):
    owner_count = lax.axis_size("blk")
    tiles_here = intensities.shape[0]
    shot_count = intensities.shape[1]
    capacity = 3 * tiles_here // owner_count
    slot_count = Q_DEV * NSEG
    slot_total = owner_count * capacity
    position = slot_positions(tile_owner, owner_count, capacity)
    placing = position[None, :] == lax.broadcasted_iota(jnp.int32, (slot_total, tiles_here), 0)
    filled = jnp.any(placing, axis=1)
    send_places = jnp.where(
        filled, jnp.sum(jnp.where(placing, tile_place[None, :], 0), axis=1), slot_count
    )
    send_pixels = (
        jnp.dot(
            placing.astype(jnp.bfloat16),
            intensities.reshape(tiles_here, shot_count * TP),
            preferred_element_type=jnp.float32,
        )
        .astype(jnp.bfloat16)
        .reshape(slot_total, shot_count, TP)
    )
    send_kernels = jnp.sum(jnp.where(placing, tile_kernel[None, :], 0), axis=1)
    outgoing_lengths = jnp.sum(jnp.where(placing, mask_len[None, :], 0), axis=1)
    got_pixels, got_kernels, got_lengths, got_places = (
        lax.all_to_all(send_pixels, "blk", split_axis=0, concat_axis=0, tiled=True),
        lax.all_to_all(send_kernels, "blk", split_axis=0, concat_axis=0, tiled=True),
        lax.all_to_all(outgoing_lengths, "blk", split_axis=0, concat_axis=0, tiled=True),
        lax.all_to_all(send_places, "blk", split_axis=0, concat_axis=0, tiled=True),
    )
    got_values, received_masks = interpolate(got_pixels, got_kernels, got_lengths, interp_weights)
    cycle_values, cycle_masks = collect_slots(got_values, received_masks, got_places, slot_count)
    cycle_rows = (
        cycle_values.reshape(Q_DEV, NSEG, shot_count, TP)
        .transpose(2, 0, 1, 3)
        .reshape(shot_count * Q_DEV, ANG)
    )
    mask_rows = cycle_masks.reshape(Q_DEV, ANG)
    next_rows = from_behind(cycle_rows[:Q_DEV], "shot", -1)
    real_part, imag_part = transform(cycle_rows, None, -1.0)
    next_real, next_imag = transform(next_rows, None, -1.0)
    after_real = jnp.concatenate([real_part[Q_DEV:], next_real], axis=0)
    after_imag = jnp.concatenate([imag_part[Q_DEV:], next_imag], axis=0)
    mask_real, mask_imaginary = transform(mask_rows, None, -1.0)
    mask_power = mask_real * mask_real + mask_imaginary * mask_imaginary
    mask_corr = transform(mask_power, None, 1.0)[0] / ANG
    denominator = jnp.maximum(jnp.maximum(mask_corr, 0.01 * mask_corr[:, :1]), 1.0)
    spectrum_power = real_part * real_part + imag_part * imag_part
    cross_real = real_part * after_real + imag_part * after_imag
    cross_imag = imag_part * after_real - real_part * after_imag
    auto_part = transform(spectrum_power, None, 1.0)[0]
    cross_part = transform(cross_real, cross_imag, 1.0)[0]
    numerator = auto_part - cross_part
    result = (numerator / ANG).reshape(shot_count, Q_DEV, ANG) / denominator[None]
    return result


def solution(mesh):
    placed = (P("blk", "shot", None), P("blk"), P("blk"), P("blk"), P("blk"), P())
    return jax.shard_map(
        per_device, mesh=mesh, in_specs=placed, out_specs=P("shot", "blk", None), check_vma=False
    )
```

profile of v0, /device:TPU:1, one launch (start us, length us, event | category | flops | bytes accessed | tf_op | source)
XLA Modules:
  0.0 122.4 jit_solution(15089146270964207235)
XLA Ops:
  0.0 0.7 fusion.152
  0.7 0.6 reduce-window.6
  1.5 0.8 fusion.125
  2.3 0.7 multiply_add_fusion.10
  3.1 1.1 select_reduce_fusion.2
  4.3 0.7 select_n.196
  5.0 9.6 %all-to-all-start = ((s32[32,24,1]{1,2,0:T(1,128)}), s32[32,24,1]{1,2,0:T(1,128)S(1)}, u32[]{:S(2)}, u32[]{:S(2)}) async-start(s32[32,24,1]{1,2,0:T(1,128)} %bitcast.12), calls=%async_computation | async-start | bytes 32768 | tf_op jit(solution)/shard_map/all_to_all | solution.py:158
  14.6 0.7 all_to_all.23
  15.3 6.2 %all-to-all-done = s32[32,24,1]{1,2,0:T(1,128)S(1)} async-done(((s32[32,24,1]{1,2,0:T(1,128)}), s32[32,24,1]{1,2,0:T(1,128)S(1)}, u32[]{:S(2)}, u32[]{:S(2)}) %all-to-all-start) | async-done | bytes 3104 | tf_op jit(solution)/shard_map/all_to_all | solution.py:158
  21.5 4.2 %all-to-all-start.3 = ((s32[32,24,1]{1,2,0:T(1,128)}), s32[32,24,1]{1,2,0:T(1,128)S(1)}, u32[]{:S(2)}, u32[]{:S(2)}) async-start(s32[32,24,1]{1,2,0:T(1,128)} %bitcast.18), calls=%async_computation.3 | async-start | bytes 32768 | tf_op jit(solution)/shard_map/all_to_all | solution.py:156
  25.6 0.7 all_to_all.20
  26.3 6.4 %all-to-all-done.3 = s32[32,24,1]{1,2,0:T(1,128)S(1)} async-done(((s32[32,24,1]{1,2,0:T(1,128)}), s32[32,24,1]{1,2,0:T(1,128)S(1)}, u32[]{:S(2)}, u32[]{:S(2)}) %all-to-all-start.3) | async-done | bytes 3104 | tf_op jit(solution)/shard_map/all_to_all | solution.py:156
  32.7 4.1 %all-to-all-start.1 = ((s32[32,24,1]{1,2,0:T(1,128)}), s32[32,24,1]{1,2,0:T(1,128)S(1)}, u32[]{:S(2)}, u32[]{:S(2)}) async-start(s32[32,24,1]{1,2,0:T(1,128)} %bitcast.15), calls=%async_computation.1 | async-start | bytes 32768 | tf_op jit(solution)/shard_map/all_to_all | solution.py:157
  36.8 1.4 %convolution_convert_fusion = bf16[768,512]{0,1:T(8,128)(2,1)S(1)} fusion(s32[256]{0:T(256)S(1)} %multiply_add_fusion.10, bf16[32,8,4,128]{3,2,1,0:T(4,128)(2,1)} %bitcast.296), kind=kOutput, calls=%fused_computation.20 | convolution fusion | flops 201916416 | bytes 1049600 | tf_op jit(solution)/shard_map/dot_general | solution.py:144
  38.2 1.3 %copy.114 = bf16[768,4,128]{2,1,0:T(4,128)(2,1)} copy(bf16[768,4,128]{0,2,1:T(8,128)(2,1)S(1)} %bitcast.290) | data formatting | bytes 1572864 | tf_op jit(solution)/shard_map/reshape | solution.py:150
  39.5 4.3 %all-to-all-done.1 = s32[32,24,1]{1,2,0:T(1,128)S(1)} async-done(((s32[32,24,1]{1,2,0:T(1,128)}), s32[32,24,1]{1,2,0:T(1,128)S(1)}, u32[]{:S(2)}, u32[]{:S(2)}) %all-to-all-start.1) | async-done | bytes 3104 | tf_op jit(solution)/shard_map/all_to_all | solution.py:157
  43.8 4.2 %all-to-all-start.2 = ((bf16[768,4,128]{2,1,0:T(4,128)(2,1)}), bf16[768,4,128]{2,1,0:T(4,128)(2,1)S(1)}, u32[]{:S(2)}, u32[]{:S(2)}) async-start(bf16[768,4,128]{2,1,0:T(4,128)(2,1)} %copy.114), calls=%async_computation.2 | async-start | bytes 1572864 | tf_op jit(solution)/shard_map/all_to_all | solution.py:155
  48.1 0.7 fusion.198
  48.8 0.5 broadcast.542
  49.4 0.7 reduce.16
  50.1 0.7 reduce.15
  50.9 0.7 reduce.14
  51.7 10.6 %all-to-all-done.2 = bf16[768,4,128]{2,1,0:T(4,128)(2,1)S(1)} async-done(((bf16[768,4,128]{2,1,0:T(4,128)(2,1)}), bf16[768,4,128]{2,1,0:T(4,128)(2,1)S(1)}, u32[]{:S(2)}, u32[]{:S(2)}) %all-to-all-start.2) | async-done | bytes 786464 | tf_op jit(solution)/shard_map/all_to_all | solution.py:155
  62.3 4.1 %while.12 = (s32[]{:T(128)}, f32[3,256,4,128]{3,2,1,0:T(4,128)S(1)}, f32[3,256,128]{2,1,0:T(8,128)S(1)}, s32[3,256]{1,0:T(4,128)S(1)}, bf16[3,256,4,128]{3,2,1,0...) while((s32[]{:T(128)}, f32[3,256,4,128]{3,2,1,0:T(4,128)S(1)}, ...), condition=%wide.region_10.11_spmd, body=%wide.region_7.10_spmd.sunk | while | flops 169117696 | bytes 3099757 | solution.py:93
  66.5 0.5 fusion.26
  67.7 1.2 fusion.73
  70.0 1.7 %convolution_bitcast_fusion = f32[4,16,16,128]{3,2,0,1:T(8,128)S(1)} fusion(f32[4,128,768,1]{2,1,0,3:T(8,128)S(1)} %bitcast.279, s32[16,16]{1,0:T(8,128)} %copy-done.8, s32[768]{0:T(1024)} %copy-done.9), kind=kOutput, calls=%fused_computation.21 | convolution fusion | flops 1208156160 | bytes 2101248 | tf_op jit(solution)/shard_map/dot_general | solution.py:118
  71.8 0.6 fusion.171
  72.4 0.6 fusion.184
  73.0 0.8 fusion.37
  73.9 1.6 %fusion.39 = f32[64,16,128]{2,1,0:T(8,128)} fusion(f32[16,64,128]{2,0,1:T(8,128)S(1)} %fusion.171, f32[16,64,128]{2,0,1:T(8,128)S(1)} %fusion.184, f32[16,128]{1,0:T(8,128)S(1)} %get-tuple-element.102, f32[16,128]{1,0:T(8,128)S(1)} %get-tuple-element.103), kind=kOutput, calls=%fused_computation.75 | convolution fusion | flops 201949184 | bytes 1589248 | tf_op jit(solution)/shard_map/rkb,bm->rkm/dot_general | solution.py:28
  76.0 0.5 fusion.20
  77.9 0.7 copy.170
  78.5 2.5 %collective-permute-start = (f32[16,2048]{1,0:T(8,128)}, f32[16,2048]{1,0:T(8,128)}, u32[]{:S(2)}, u32[]{:S(2)}) collective-permute-start(f32[16,2048]{1,0:T(8,128)} %bitcast.257), channel_id=1, source_target_pairs={{32,0},{64,32},{96,64},{0,96},{33,1},{65,33},{97,65},{1,97},{34,2}... | collective-permute-start | bytes 393224 | tf_op jit(solution)/shard_map/ppermute | solution.py:17
  81.0 0.8 fusion.13
  83.3 0.6 div.35
  84.0 0.7 maximum_maximum_fusion
  84.7 1.9 %fusion.14 = f32[64,128,16]{1,2,0:T(8,128)S(1)} fusion(f32[64,16,128]{2,1,0:T(8,128)} %fusion.39, f32[16,64,128]{2,0,1:T(8,128)S(1)} %fusion.171, f32[16,64,128]{2,0,1:T(8,128)S(1)} %fusion.184, f32[16,128]{1,0:T(8,128)S(1)} %get-tuple-element.102, f32[16,128]{1,0:T(8,128)S(1)} %get-tuple-element.103), kind=kOutput, calls=%fused_computation.32 | convolution fusion | flops 202096640 | bytes 2113536 | tf_op jit(solution)/shard_map/rkb,bm->rkm/dot_general | solution.py:28
  86.6 0.6 copy.122
  87.2 0.8 slice.31
  88.0 0.6 copy.121
  88.6 1.5 %copy.125 = f32[48,128,16]{0,2,1:T(8,128)S(1)} copy(f32[48,128,16]{1,2,0:T(8,128)} %slice.31) | data formatting | bytes 786432 | tf_op jit(solution)/shard_map/slice | solution.py:171
  90.1 1.4 %copy.128 = f32[48,128,16]{0,2,1:T(8,128)} copy(f32[48,128,16]{1,2,0:T(8,128)S(1)} %slice-done) | data formatting | bytes 786432 | tf_op jit(solution)/shard_map/slice | solution.py:172
  91.6 0.9 copy.154
  93.1 0.5 fusion.79
  94.7 0.5 fusion.18
  95.2 1.4 %copy.143 = f32[16,128,16]{0,2,1:T(8,128)} copy(f32[16,128,16]{1,2,0:T(8,128)S(1)} %fusion.18) | data formatting | bytes 262144 | tf_op jit(solution)/shard_map/concatenate | solution.py:171
  96.6 1.4 %copy.144 = f32[16,128,16]{0,2,1:T(8,128)} copy(f32[16,128,16]{1,2,0:T(8,128)S(1)} %fusion.17) | data formatting | bytes 262144 | tf_op jit(solution)/shard_map/concatenate | solution.py:172
  98.1 4.2 %fusion.25 = (f32[64,16,128]{0,2,1:T(8,128)}, f32[64,16,128]{0,2,1:T(8,128)}, f32[64,16,128]{0,2,1:T(8,128)}) fusion(f32[16,16,128]{0,2,1:T(8,128)} %bitcast.289, f32[48,16,128]{0,2,1:T(8,128)} %bitcast.287, f32[16,16,128]{0,2,1:T(8,128)} %bitcast.288, f32[48,16,128]{0,2,1:T(8,128)S(1)} %bitcast.286, f32[64,16,128]{0,2,1:T(8,128)S(1)} %bitcast.284, ...), kind=kLoop, calls=%fused_computation.53 | loop fusion | flops 1441792 | bytes 3670016 | tf_op jit(solution)/shard_map/sub | solution.py:179
  102.3 1.6 %copy.123 = f32[64,16,128]{2,1,0:T(8,128)S(1)} copy(f32[64,16,128]{0,2,1:T(8,128)} %get-tuple-element.101) | data formatting | bytes 1048576 | tf_op jit(solution)/shard_map/add | solution.py:177
  103.9 0.6 fusion.165
  104.5 0.6 fusion.182
  105.2 1.7 %copy.131 = f32[64,16,128]{2,1,0:T(8,128)S(1)} copy(f32[64,16,128]{0,2,1:T(8,128)} %get-tuple-element.100) | data formatting | bytes 1048576 | tf_op jit(solution)/shard_map/add | solution.py:178
  106.9 1.4 %fusion.162 = f32[16,64,128]{2,0,1:T(8,128)} fusion(f32[64,16,128]{2,1,0:T(8,128)S(1)} %copy.131), kind=kOutput, calls=%fused_computation.204 | convolution fusion | flops 25169408 | bytes 1048576 | tf_op jit(solution)/shard_map/rab,ak->rkb/dot_general | solution.py:28
  108.3 0.9 fusion.178
  109.6 0.8 fusion.33
  110.4 0.8 convolution_subtract_fusion.2
  111.3 0.6 convolution_add_fusion
  111.9 0.6 convolution_subtract_fusion.1
  112.5 0.8 fusion.30
  113.3 0.8 fusion.12
  114.2 2.6 %copy.135 = f32[64,128,16]{2,1,0:T(8,128)} copy(f32[64,128,16]{1,2,0:T(8,128)S(1)} %fusion.12) | data formatting | bytes 1048576 | tf_op jit(solution)/shard_map/div | solution.py:183
  116.8 4.7 %div.31 = f32[4,16,2048]{2,1,0:T(8,128)S(1)} reshape(f32[64,128,16]{2,1,0:T(8,128)} %copy.135) | data formatting | bytes 1048576 | tf_op jit(solution)/shard_map/div | solution.py:183
  121.5 0.8 broadcast_divide_fusion
  (84 shorter events, 11.8 us)
Async XLA Ops:
  5.0 16.5 %all-to-all-start = ((s32[32,24,1]{1,2,0:T(1,128)}), s32[32,24,1]{1,2,0:T(1,128)S(1)}, u32[]{:S(2)}, u32[]{:S(2)}) async-start(s32[32,24,1]{1,2,0:T(1,128)} %bitcast.12), calls=%async_computation | async-start | bytes 32768 | tf_op jit(solution)/shard_map/all_to_all | solution.py:158
  21.5 11.2 %all-to-all-start.3 = ((s32[32,24,1]{1,2,0:T(1,128)}), s32[32,24,1]{1,2,0:T(1,128)S(1)}, u32[]{:S(2)}, u32[]{:S(2)}) async-start(s32[32,24,1]{1,2,0:T(1,128)} %bitcast.18), calls=%async_computation.3 | async-start | bytes 32768 | tf_op jit(solution)/shard_map/all_to_all | solution.py:156
  32.7 11.1 %all-to-all-start.1 = ((s32[32,24,1]{1,2,0:T(1,128)}), s32[32,24,1]{1,2,0:T(1,128)S(1)}, u32[]{:S(2)}, u32[]{:S(2)}) async-start(s32[32,24,1]{1,2,0:T(1,128)} %bitcast.15), calls=%async_computation.1 | async-start | bytes 32768 | tf_op jit(solution)/shard_map/all_to_all | solution.py:157
  38.2 24.1 %copy-start.10 = (bf16[4,128,128]{2,1,0:T(8,128)(2,1)S(1)}, bf16[4,128,128]{2,1,0:T(8,128)(2,1)}, u32[]{:S(2)}) copy-start(bf16[4,128,128]{2,1,0:T(8,128)(2,1)} %param.13) | copy-start | bytes 393220
  43.8 18.6 %all-to-all-start.2 = ((bf16[768,4,128]{2,1,0:T(4,128)(2,1)}), bf16[768,4,128]{2,1,0:T(4,128)(2,1)S(1)}, u32[]{:S(2)}, u32[]{:S(2)}) async-start(bf16[768,4,128]{2,1,0:T(4,128)(2,1)} %copy.114), calls=%async_computation.2 | async-start | bytes 1572864 | tf_op jit(solution)/shard_map/all_to_all | solution.py:155
  48.1 18.4 %copy-start.8 = (s32[16,16]{1,0:T(8,128)}, s32[16,16]{1,0:T(8,128)S(1)}, u32[]{:S(2)}) copy-start(s32[16,16]{1,0:T(8,128)S(1)} %copy.112) | copy-start | bytes 3076
  50.1 16.4 %copy-start.9 = (s32[768]{0:T(1024)}, s32[768]{0:T(1024)S(1)}, u32[]{:S(2)}) copy-start(s32[768]{0:T(1024)S(1)} %eq.87) | copy-start | bytes 9220
  71.7 1.3 %copy-start.2 = (f32[4,16,16,128]{3,2,0,1:T(8,128)}, f32[4,16,16,128]{3,2,0,1:T(8,128)S(1)}, u32[]{:S(2)}) copy-start(f32[4,16,16,128]{3,2,0,1:T(8,128)S(1)} %convolution_bitcast_fusion) | copy-start | bytes 1572868
  73.0 2.5 %copy-start.5 = (f32[16,16,128]{2,1,0:T(8,128)S(1)}, f32[16,16,128]{2,1,0:T(8,128)}, u32[]{:S(2)}) copy-start(f32[16,16,128]{2,1,0:T(8,128)} %fusion.73) | copy-start | bytes 393220
  76.5 1.3 %slice-start.1 = ((f32[4,16,16,128]{3,2,0,1:T(8,128)}), f32[1,16,16,128]{3,2,0,1:T(8,128)S(1)}, s32[]{:S(2)}) async-start(f32[4,16,16,128]{3,2,0,1:T(8,128)} %copy-done.2), calls=%async_computation.5 | async-start | bytes 262144 | tf_op jit(solution)/shard_map/slice | solution.py:168
  77.2 4.7 %copy-start.6 = (f32[16,128]{1,0:T(8,128)S(1)}, f32[16,128]{1,0:T(8,128)}, u32[]{:S(2)}) copy-start(f32[16,128]{1,0:T(8,128)} %fusion.198) | copy-start | bytes 24580
  78.5 13.0 %collective-permute-start = (f32[16,2048]{1,0:T(8,128)}, f32[16,2048]{1,0:T(8,128)}, u32[]{:S(2)}, u32[]{:S(2)}) collective-permute-start(f32[16,2048]{1,0:T(8,128)} %bitcast.257), channel_id=1, source_target_pairs={{32,0},{64,32},{96,64},{0,96},{33,1},{65,33},{97,65},{1,97},{34,2}... | collective-permute-start | bytes 393224 | tf_op jit(solution)/shard_map/ppermute | solution.py:17
  81.9 4.7 %copy-start.1 = (f32[64,128,16]{1,2,0:T(8,128)}, f32[64,128,16]{1,2,0:T(8,128)S(1)}, u32[]{:S(2)}) copy-start(f32[64,128,16]{1,2,0:T(8,128)S(1)} %fusion.13) | copy-start | bytes 1572868
  88.0 2.1 %slice-start = ((f32[64,128,16]{1,2,0:T(8,128)}), f32[48,128,16]{1,2,0:T(8,128)S(1)}, s32[]{:S(2)}) async-start(f32[64,128,16]{1,2,0:T(8,128)} %copy-done.1), calls=%async_computation.4 | async-start | bytes 786432 | tf_op jit(solution)/shard_map/slice | solution.py:172
  105.2 4.0 %copy-start = (f32[64,16,128]{0,2,1:T(8,128)S(1)}, f32[64,16,128]{0,2,1:T(8,128)}, u32[]{:S(2)}) copy-start(f32[64,16,128]{0,2,1:T(8,128)} %get-tuple-element.99) | copy-start | bytes 1572868
  108.3 1.3 %copy-start.7 = (f32[16,128]{1,0:T(8,128)S(1)}, f32[16,128]{1,0:T(8,128)}, u32[]{:S(2)}) copy-start(f32[16,128]{1,0:T(8,128)} %fusion.198) | copy-start | bytes 24580
  109.6 1.7 %copy-start.3 = (f32[16,64,128]{2,0,1:T(8,128)S(1)}, f32[16,64,128]{2,0,1:T(8,128)}, u32[]{:S(2)}) copy-start(f32[16,64,128]{2,0,1:T(8,128)} %fusion.162) | copy-start | bytes 1572868
  116.8 4.7 %copy-start.4 = (f32[16,2048]{1,0:T(8,128)S(1)}, f32[16,2048]{1,0:T(8,128)}, u32[]{:S(2)}) copy-start(f32[16,2048]{1,0:T(8,128)} %maximum_maximum_fusion) | copy-start | bytes 393220
where the time goes:
time: 123 us; the launch traced here: 122 us
  local copies, waits for them, and re-layouts  28.5 us (23%)
  matrix products  27.8 us (23%)
  waiting for transfers between devices  27.5 us (22%)
  starting transfers between devices  24.6 us (20%)
  other arithmetic  13.1 us (11%)
    dot_general x32, matrix products, contract(): jnp.einsum(form, first_array, second_array, precision=lax.Precision.HIGHE...  22 us
    all_to_all x1, waiting for transfers between devices, per_device(): lax.all_to_all(send_pixels, 'blk', split_axis=0, concat_axis=0, tiled=True)  10.6 us
    all_to_all x1, starting transfers between devices, per_device(): lax.all_to_all(send_places, 'blk', split_axis=0, concat_axis=0, tiled=True)  9.6 us
    div x2, local copies, waits for them, and re-layouts, per_device(): numerator / ANG  7.33 us
    all_to_all x1, waiting for transfers between devices, per_device(): lax.all_to_all(send_kernels, 'blk', split_axis=0, concat_axis=0, tiled=True)  6.36 us
    all_to_all x1, waiting for transfers between devices, per_device(): lax.all_to_all(send_places, 'blk', split_axis=0, concat_axis=0, tiled=True)  6.18 us
    all_to_all x1, waiting for transfers between devices, per_device(): lax.all_to_all(outgoing_lengths, 'blk', split_axis=0, concat_axis=0, tile...  4.28 us
    sub x1, other arithmetic, per_device(): cross_imag = imag_part * after_real - real_part * after_imag  4.24 us
  transfers between devices with their start and end apart: 5, of which 4 were waited for; matrix products, arithmetic and copies ran while one was open for 14% of the time, Pallas kernels for 0%

commit v1 on v0

v1 whole, which is shorter than its diff:
```python
import functools
import math

import jax
import jax.numpy as jnp
import numpy as np
from jax import lax
from jax.experimental import pallas as pl
from jax.experimental.pallas import tpu as pltpu
from jax.sharding import PartitionSpec as P

ANG = 2048
TP = 128
Q_DEV = 16
NSEG = 16
HALF = NSEG // 2
FREQS = HALF + 1
ROWS = FREQS * Q_DEV
FIELD = 32
GROUP = 4
MESH = pl.DeviceIdType.MESH


def dft_tables():
    b = np.arange(TP)
    angle = 2.0 * math.pi * (np.outer(b, b) % TP) / TP
    cos, sin = np.cos(angle), np.sin(angle)
    table = np.block([[cos, -sin], [sin, cos]]).astype(np.float32)
    high = table.astype(jnp.bfloat16)
    low = (table - high.astype(np.float32)).astype(jnp.bfloat16)
    dft = np.concatenate([high, high, low], axis=0)
    twist = 2.0 * math.pi * (np.outer(np.arange(FREQS), b) % ANG) / ANG
    scale = np.full((FREQS, 1), 2.0 / ANG)
    scale[0] = scale[HALF] = 1.0 / ANG
    turns = np.stack(
        [np.cos(twist), -np.sin(twist), scale * np.cos(twist), -scale * np.sin(twist)]
    ).astype(np.float32)
    return dft, turns


def cosine_sums(first, middle, rest):
    c1, c3, r2 = math.cos(math.pi / 8), math.cos(3 * math.pi / 8), math.sqrt(0.5)
    even, odd = first + middle, first - middle
    g, h = rest[2] + rest[6], r2 * (rest[2] - rest[6])
    base = even + rest[4]
    p = [base + g, odd + h, even - rest[4], odd - h, base - g]
    u1, u3 = rest[1] - rest[7], rest[3] - rest[5]
    t1, t3 = rest[1] + rest[7], rest[3] + rest[5]
    q = [t1 + t3, c1 * u1 + c3 * u3, r2 * (t1 - t3), c3 * u1 - c1 * u3]
    low = [p[k] + q[k] for k in range(4)]
    high = [p[k] - q[k] for k in range(3, -1, -1)]
    return low + [p[4]] + high


def sine_sums(v):
    c1, c3, r2 = math.cos(math.pi / 8), math.cos(3 * math.pi / 8), math.sqrt(0.5)
    e = r2 * (v[2] + v[6])
    w = [None, e + v[4], v[2] - v[6], e - v[4]]
    a, b = v[1] + v[7], v[3] + v[5]
    s, t = v[1] - v[7], v[3] - v[5]
    o = [None, c3 * a + c1 * b, r2 * (s + t), c1 * a - c3 * b]
    low = [o[k] + w[k] for k in range(1, 4)]
    high = [o[k] - w[k] for k in range(3, 0, -1)]
    return [None] + low + [s - t] + high


def split(x):
    high = x.astype(jnp.bfloat16)
    return high, (x - high.astype(jnp.float32)).astype(jnp.bfloat16)


def dot(a, b, rhs_dim=0):
    return lax.dot_general(
        a, b, (((1,), (rhs_dim,)), ((), ())), preferred_element_type=jnp.float32
    )


def kernel(
    owners, cap, shots, shot_blocks,
    pix_ref, owner_ref, place_ref, kind_ref, len_ref, weights_ref, dft_ref, turns_ref,
    out_ref,
    wide, send, recv, meta, meta_send, meta_recv, place_col, kind_col, len_col,
    chosen, values, cycles, halo, high, low, spectra, inverse,
    send_sem, recv_sem, meta_send_sem, meta_recv_sem, halo_sem,
):
    me, block = lax.axis_index("blk"), lax.axis_index("shot")
    tiles = owner_ref.shape[1]
    rows = cap * shots
    bf16, f32 = jnp.bfloat16, jnp.float32
    left = lax.rem(block + shot_blocks - 1, shot_blocks)
    right = lax.rem(block + 1, shot_blocks)

    barrier = pltpu.get_barrier_semaphore()

    def greet(i, carry):
        pl.semaphore_signal(
            barrier, inc=1, device_id=(block, lax.rem(me + i, owners)), device_id_type=MESH
        )
        return carry

    lax.fori_loop(1, owners, greet, 0)
    pl.semaphore_signal(barrier, inc=1, device_id=(right, me), device_id_type=MESH)

    relative = lax.rem(owner_ref[...] - me + owners, owners)
    goes = lax.broadcasted_iota(jnp.int32, (owners, tiles), 0) == relative
    goes_bf = goes.astype(f32).astype(bf16)
    before = (
        lax.broadcasted_iota(jnp.int32, (tiles, tiles), 0)
        < lax.broadcasted_iota(jnp.int32, (tiles, tiles), 1)
    ).astype(f32).astype(bf16)
    earlier = dot(goes_bf, before)
    rank = jnp.sum(jnp.where(goes, earlier, 0.0), axis=0, keepdims=True)
    position = relative.astype(f32) * cap + rank

    place = place_ref[...]
    place = lax.rem(place, NSEG) * Q_DEV + lax.div(place, NSEG)
    at_rank = lax.broadcasted_iota(jnp.int32, (FIELD, tiles), 0).astype(f32) == rank
    fields = [
        jnp.where(at_rank, jnp.broadcast_to(f.astype(f32), at_rank.shape), 0.0)
        for f in (place, kind_ref[...], len_ref[...])
    ]
    fields = jnp.concatenate(fields + [jnp.zeros((FIELD, tiles), f32)], axis=0).astype(bf16)
    meta[...] = dot(goes_bf, fields, 1)

    def lay_meta(i, carry):
        meta_send[i] = meta[pl.ds(i, 1), :]
        return carry

    lax.fori_loop(0, owners, lay_meta, 0)
    meta_recv[0] = meta_send[0]

    wide[...] = pix_ref[...].astype(f32)
    lengths = len_ref[...].astype(f32)
    lengths = jnp.concatenate(
        [
            jnp.transpose(jnp.broadcast_to(lengths[:, i : i + TP], (TP, TP)))
            for i in range(0, tiles, TP)
        ],
        axis=0,
    )
    live = lax.broadcasted_iota(jnp.int32, (tiles, TP), 1).astype(f32) < lengths
    masked = jnp.concatenate(
        [
            jnp.where(live, wide[pl.ds(s, tiles, stride=shots), :], 0.0).astype(bf16)
            for s in range(shots)
        ],
        axis=1,
    )

    per = 8

    def pack(c, carry):
        spot = lax.broadcasted_iota(jnp.int32, (per * cap, tiles), 0) + c * (per * cap)
        placing = (spot.astype(f32) == position).astype(f32).astype(bf16)
        packed = dot(placing, masked)
        for d in range(per):
            mine = packed[d * cap : (d + 1) * cap]
            mine = jnp.concatenate([mine[:, s * TP : (s + 1) * TP] for s in range(shots)], axis=0)
            send[c * per + d] = mine.astype(bf16)
        return carry

    lax.fori_loop(0, owners // per, pack, 0)
    recv[0] = send[0]

    pl.semaphore_wait(barrier, owners)

    def meta_copy(i):
        return pltpu.make_async_remote_copy(
            src_ref=meta_send.at[i], dst_ref=meta_recv.at[i],
            send_sem=meta_send_sem, recv_sem=meta_recv_sem,
            device_id=(block, lax.rem(me + i, owners)), device_id_type=MESH,
        )

    def pixel_copy(i, g):
        return pltpu.make_async_remote_copy(
            src_ref=send.at[i], dst_ref=recv.at[i],
            send_sem=send_sem, recv_sem=recv_sem.at[g],
            device_id=(block, lax.rem(me + i, owners)), device_id_type=MESH,
        )

    def start_meta(i, carry):
        meta_copy(i).start()
        return carry

    def start_pixels(i, carry):
        pixel_copy(i, lax.div(i, GROUP)).start()
        return carry

    lax.fori_loop(1, owners, start_meta, 0)
    lax.fori_loop(1, owners, start_pixels, 0)

    others = pl.ds(1, owners - 1)
    all_meta = pltpu.make_async_remote_copy(
        src_ref=meta_send.at[others], dst_ref=meta_recv.at[others],
        send_sem=meta_send_sem, recv_sem=meta_recv_sem,
        device_id=(block, lax.rem(me + 1, owners)), device_id_type=MESH,
    )
    all_meta.wait_recv()

    def columns(i, carry):
        turned = jnp.transpose(jnp.broadcast_to(meta_recv[i], (TP, TP)))
        here = pl.ds(pl.multiple_of(i * cap, 8), cap)
        place_col[here, :] = turned[0:cap]
        kind_col[here, :] = turned[FIELD : FIELD + cap]
        len_col[here, :] = turned[2 * FIELD : 2 * FIELD + cap]
        return carry

    lax.fori_loop(0, owners, columns, 0)

    slots = Q_DEV * NSEG
    slot = lax.broadcasted_iota(jnp.int32, (slots, TP), 0).astype(f32)
    for i in range(owners * cap // TP):
        line = jnp.transpose(place_col[i * TP : (i + 1) * TP, :])
        line = jnp.broadcast_to(line[0:1], (slots, TP))
        chosen[:, i * TP : (i + 1) * TP] = (slot == line).astype(f32).astype(bf16)

    weights = jnp.concatenate([weights_ref[k] for k in range(weights_ref.shape[0])], axis=1)
    kinds = weights_ref.shape[0]

    def pick(kind, product):
        picked = product[:, 0:TP]
        for k in range(1, kinds):
            picked = jnp.where(kind == float(k), product[:, k * TP : (k + 1) * TP], picked)
        return picked

    span = GROUP * cap

    def interpolate(g, carry):
        here = pl.ds(pl.multiple_of(g * span, 16), span)
        kind = kind_col[here, :]

        pixels = recv[pl.ds(g * GROUP, GROUP)].reshape(GROUP * rows, TP)
        product = dot(pixels, weights)
        for s in range(shots):
            mine = jnp.concatenate(
                [
                    product[i * rows + s * cap : i * rows + (s + 1) * cap]
                    for i in range(GROUP)
                ],
                axis=0,
            )
            hi, lo = split(pick(kind, mine))
            values[here, 2 * s * TP : (2 * s + 1) * TP] = hi
            values[here, (2 * s + 1) * TP : (2 * s + 2) * TP] = lo
        return carry

    def interpolate_live(g, carry):
        here = pl.ds(pl.multiple_of(g * span, 16), span)
        kind = kind_col[here, :]
        pixel = lax.broadcasted_iota(jnp.int32, (span, TP), 1).astype(f32)
        alive = (pixel < len_col[here, :]).astype(f32).astype(bf16)
        hi, lo = split(pick(kind, dot(alive, weights)))
        values[here, 2 * shots * TP : (2 * shots + 1) * TP] = hi
        values[here, (2 * shots + 1) * TP : (2 * shots + 2) * TP] = lo
        return carry

    def wait_group(first, count, g):
        these = pl.ds(first, count)
        pltpu.make_async_remote_copy(
            src_ref=send.at[these], dst_ref=recv.at[these],
            send_sem=send_sem, recv_sem=recv_sem.at[g],
            device_id=(block, lax.rem(me + 1, owners)), device_id_type=MESH,
        ).wait_recv()

    lax.fori_loop(0, owners // GROUP, interpolate_live, 0)
    wait_group(1, GROUP - 1, 0)
    interpolate(0, 0)

    def receive(g, carry):
        wait_group(g * GROUP, GROUP, g)
        return interpolate(g, carry)

    lax.fori_loop(1, owners // GROUP, receive, 0)

    def gather(s):
        both = dot(chosen[...], values[:, 2 * s * TP : (2 * s + 2) * TP])
        cycles[s] = both[:, :TP] + both[:, TP:]

    gather(0)
    halo_copy = pltpu.make_async_remote_copy(
        src_ref=cycles.at[0], dst_ref=halo,
        send_sem=halo_sem.at[0], recv_sem=halo_sem.at[1],
        device_id=(left, me), device_id_type=MESH,
    )
    halo_copy.start()
    for s in range(1, shots + 1):
        gather(s)

    def put(here, real, imag):
        for j, part in enumerate((real, imag)):
            hi, lo = split(part)
            high[here, j * TP : (j + 1) * TP] = hi
            low[here, j * TP : (j + 1) * TP] = lo

    def forward(ref, s, carry):
        x = [ref[pl.ds(a * Q_DEV, Q_DEV), :] for a in range(NSEG)]
        total = [None] + [x[a] + x[NSEG - a] for a in range(1, HALF)]
        differ = [None] + [x[a] - x[NSEG - a] for a in range(1, HALF)]
        real = cosine_sums(x[0], x[HALF], total)
        imag = sine_sums(differ)
        for k in range(FREQS):
            here = pl.ds(pl.multiple_of(s * ROWS + k * Q_DEV, 16), Q_DEV)
            cos, sin = turns_ref[0, k : k + 1, :], turns_ref[1, k : k + 1, :]
            if k == 0:
                put(here, real[k], jnp.zeros_like(real[k]))
            elif k == HALF:
                put(here, real[k] * cos, real[k] * sin)
            else:
                put(here, real[k] * cos + imag[k] * sin, real[k] * sin - imag[k] * cos)
        return carry

    def transform(first, count):
        here = pl.ds(first * ROWS, count * ROWS)
        hi, lo = high[here, :], low[here, :]
        return dot(jnp.concatenate([hi, lo, hi], axis=1), dft_ref[...])

    def correlate(s, following, target):
        for k in range(FREQS):
            def at(i):
                return pl.ds(pl.multiple_of(i * ROWS + k * Q_DEV, 16), Q_DEV)
            mine = spectra[at(s), :]
            xr, xi = mine[:, :TP], mine[:, TP:]
            if following is None:
                fr, fi = xr * xr + xi * xi, jnp.zeros_like(xr)
            else:
                differ = mine - spectra[at(following), :]
                dr, di = differ[:, :TP], differ[:, TP:]
                fr, fi = xr * dr + xi * di, xr * di - xi * dr
            put(at(target), fr, fi)

    def back(s):
        parts = []
        for k in range(FREQS):
            here = pl.ds(pl.multiple_of(s * ROWS + k * Q_DEV, 16), Q_DEV)
            re, im = inverse[here, :TP], inverse[here, TP:]
            cos, sin = turns_ref[2, k : k + 1, :], turns_ref[3, k : k + 1, :]
            parts.append((re * cos - im * sin, re * sin + im * cos))
        sums = cosine_sums(parts[0][0], parts[HALF][0], [p[0] for p in parts])
        turned = sine_sums([p[1] for p in parts])
        found = [None] * NSEG
        found[0], found[HALF] = sums[0], sums[HALF]
        for a in range(1, HALF):
            found[a], found[NSEG - a] = sums[a] + turned[a], sums[a] - turned[a]
        return found

    lax.fori_loop(0, shots + 1, lambda s, c: forward(cycles.at[s], s, c), 0)
    spectra[0 : (shots + 1) * ROWS, :] = transform(0, shots + 1)

    def correlate_shot(s, carry):
        correlate(s, s + 1, s)
        return carry

    lax.fori_loop(0, shots - 1, correlate_shot, 0)
    correlate(shots, None, shots - 1)
    inverse[0 : shots * ROWS, :] = transform(0, shots)

    mask = back(shots - 1)
    floor = jnp.maximum(0.01 * mask[0][:, 0:1], 1.0)
    for a in range(NSEG):
        cycles[shots, a * Q_DEV : (a + 1) * Q_DEV, :] = 1.0 / jnp.maximum(mask[a], floor)

    def finish(s, source):
        found = back(source)
        for a in range(NSEG):
            share = cycles[shots, a * Q_DEV : (a + 1) * Q_DEV, :]
            out_ref[s, :, a * TP : (a + 1) * TP] = found[a] * share

    def finish_shot(s, carry):
        finish(s, s)
        return carry

    lax.fori_loop(0, shots - 1, finish_shot, 0)

    halo_copy.wait_recv()
    forward(halo, 0, 0)
    spectra[shots * ROWS : (shots + 1) * ROWS, :] = transform(0, 1)
    correlate(shots - 1, shots, 0)
    inverse[0:ROWS, :] = transform(0, 1)
    finish(shots - 1, 0)

    halo_copy.wait_send()
    all_meta.wait_send()
    pltpu.make_async_remote_copy(
        src_ref=send.at[others], dst_ref=recv.at[others],
        send_sem=send_sem, recv_sem=recv_sem.at[0],
        device_id=(block, lax.rem(me + 1, owners)), device_id_type=MESH,
    ).wait_send()


def per_device(intensities, tile_owner, tile_place, tile_kernel, mask_len, interp_weights):
    owners, shot_blocks = lax.axis_size("blk"), lax.axis_size("shot")
    tiles, shots, _ = intensities.shape
    cap = 3 * tiles // owners
    dft, turns = dft_tables()
    bf16, f32 = jnp.bfloat16, jnp.float32
    slots = Q_DEV * NSEG
    return pl.pallas_call(
        functools.partial(kernel, owners, cap, shots, shot_blocks),
        out_shape=jax.ShapeDtypeStruct((shots, Q_DEV, ANG), f32),
        in_specs=[pl.BlockSpec(memory_space=pltpu.VMEM)] * 8,
        out_specs=pl.BlockSpec(memory_space=pltpu.VMEM),
        scratch_shapes=[
            pltpu.VMEM((tiles * shots, TP), f32),
            pltpu.VMEM((owners, cap * shots, TP), bf16),
            pltpu.VMEM((owners, cap * shots, TP), bf16),
            pltpu.VMEM((owners, TP), f32),
            pltpu.VMEM((owners, 1, TP), f32),
            pltpu.VMEM((owners, 1, TP), f32),
            pltpu.VMEM((owners * cap, TP), f32),
            pltpu.VMEM((owners * cap, TP), f32),
            pltpu.VMEM((owners * cap, TP), f32),
            pltpu.VMEM((slots, owners * cap), bf16),
            pltpu.VMEM((owners * cap, (shots + 1) * 2 * TP), bf16),
            pltpu.VMEM((shots + 1, slots, TP), f32),
            pltpu.VMEM((slots, TP), f32),
            pltpu.VMEM(((shots + 1) * ROWS, 2 * TP), bf16),
            pltpu.VMEM(((shots + 1) * ROWS, 2 * TP), bf16),
            pltpu.VMEM(((shots + 1) * ROWS, 2 * TP), f32),
            pltpu.VMEM((shots * ROWS, 2 * TP), f32),
            pltpu.SemaphoreType.DMA,
            pltpu.SemaphoreType.DMA((owners // GROUP,)),
            pltpu.SemaphoreType.DMA,
            pltpu.SemaphoreType.DMA,
            pltpu.SemaphoreType.DMA((2,)),
        ],
        compiler_params=pltpu.CompilerParams(
            collective_id=0, has_side_effects=True, vmem_limit_bytes=40 * 2**20
        ),
        cost_estimate=pl.CostEstimate(
            flops=3 * 10**9, bytes_accessed=2 * 10**6, transcendentals=0
        ),
    )(
        intensities.reshape(tiles * shots, TP),
        tile_owner.reshape(1, tiles),
        tile_place.reshape(1, tiles),
        tile_kernel.reshape(1, tiles),
        mask_len.reshape(1, tiles),
        interp_weights,
        jnp.asarray(dft),
        jnp.asarray(turns),
    )


def solution(mesh):
    placed = (P("blk", "shot", None), P("blk"), P("blk"), P("blk"), P("blk"), P())
    return jax.shard_map(
        per_device, mesh=mesh, in_specs=placed, out_specs=P("shot", "blk", None), check_vma=False
    )
```

time: 123 us -> 32.9 us (0.27)
  the two profiles are of different devices: /device:TPU:1 before, /device:TPU:10 now
where the time goes in v1:
time: 32.9 us; the launch traced here: 32.6 us
  Pallas kernels  27.5 us (84%)
  local copies, waits for them, and re-layouts  5.11 us (16%)
    pallas_call x1, Pallas kernels, per_device(): pl.pallas_call(functools.partial(kernel, owners, cap, shots, shot_blocks)...  27.5 us
    unnamed x17, local copies, waits for them, and re-layouts  5.11 us

profile of v1, /device:TPU:10, one launch (start us, length us, event | category | flops | bytes accessed | tf_op | source)
XLA Modules:
  0.0 32.6 jit_solution(12878150679080554637)
XLA Ops:
  0.0 0.0 copy-start.5
  0.0 0.0 copy-start.3
  0.0 0.0 copy-start.4
  0.0 0.0 copy-start.2
  0.0 0.7 %copy-done.5 = s32[256]{0:T(256)S(1)} copy-done((s32[256]{0:T(256)S(1)}, s32[256]{0:T(256)}, u32[]{:S(2)}) %copy-start.5) | copy-done | bytes 1048
  0.7 0.0 copy-done.3
  0.7 0.0 copy-done.4
  0.7 0.0 copy-done.2
  0.7 0.0 copy-start
  0.7 0.9 %copy-done = bf16[256,4,128]{2,1,0:T(4,128)(2,1)S(1)} copy-done((bf16[256,4,128]{2,1,0:T(4,128)(2,1)S(1)}, bf16[256,4,128]{2,1,0:T(4,128)(2,1)}, u32[]{:S(2)}) %copy-start) | copy-done | bytes 262168
  1.7 0.0 copy-start.1
  1.7 0.9 %copy-done.1 = bf16[4,128,128]{2,1,0:T(8,128)(2,1)S(1)} copy-done((bf16[4,128,128]{2,1,0:T(8,128)(2,1)S(1)}, bf16[4,128,128]{2,1,0:T(8,128)(2,1)}, u32[]{:S(2)}) %copy-start.1) | copy-done | bytes 131096
  2.6 0.0 copy-start.6
  2.6 1.0 %copy-done.6 = bf16[768,256]{1,0:T(8,128)(2,1)S(1)} copy-done((bf16[768,256]{1,0:T(8,128)(2,1)S(1)}, bf16[768,256]{1,0:T(8,128)(2,1)}, u32[]{:S(2)}) %copy-start.6) | copy-done | bytes 393240
  3.6 0.0 copy-start.7
  3.6 0.8 %copy-done.7 = f32[4,9,128]{2,1,0:T(8,128)S(1)} copy-done((f32[4,9,128]{2,1,0:T(8,128)S(1)}, f32[4,9,128]{2,1,0:T(8,128)}, u32[]{:S(2)}) %copy-start.7) | copy-done | bytes 18456
  4.3 27.5 %shard_map.82 = f32[4,16,2048]{2,1,0:T(8,128)S(1)} custom-call(bf16[1024,128]{1,0:T(8,128)(2,1)S(1)} %bitcast.5, s32[1,256]{1,0:T(1,128)S(1)} %bitcast.6, s32[1,256]{1,0:T(1,128)S(1)} %bitcast.7, s32[1,256]{1,0:T(1,128)S(1)} %bitcast.8, s32[1,256]{1,0:T(1,128)S(1)} %bitcast.9, bf16[4,128,128]{2,1,0:T(8,128)(2,1)S(1)} %copy-done.1, ...), custom_call_target="tpu_custom_call" | custom-call | flops 3000000000 | bytes 2000000 | tf_op jit(solution)/shard_map/pallas_call | solution.py:397
  31.8 0.8 %copy.10 = f32[4,16,2048]{2,1,0:T(8,128)} copy(f32[4,16,2048]{2,1,0:T(8,128)S(1)} %shard_map.82) | data formatting | bytes 1048576
Async XLA Ops:
  0.0 0.7 %copy-start.5 = (s32[256]{0:T(256)S(1)}, s32[256]{0:T(256)}, u32[]{:S(2)}) copy-start(s32[256]{0:T(256)} %param.12) | copy-start | bytes 3076
  0.0 0.7 %copy-start.3 = (s32[256]{0:T(256)S(1)}, s32[256]{0:T(256)}, u32[]{:S(2)}) copy-start(s32[256]{0:T(256)} %param.10) | copy-start | bytes 3076
  0.0 0.7 %copy-start.4 = (s32[256]{0:T(256)S(1)}, s32[256]{0:T(256)}, u32[]{:S(2)}) copy-start(s32[256]{0:T(256)} %param.11) | copy-start | bytes 3076
  0.0 0.7 %copy-start.2 = (s32[256]{0:T(256)S(1)}, s32[256]{0:T(256)}, u32[]{:S(2)}) copy-start(s32[256]{0:T(256)} %param.9) | copy-start | bytes 3076
  0.7 0.9 %copy-start = (bf16[256,4,128]{2,1,0:T(4,128)(2,1)S(1)}, bf16[256,4,128]{2,1,0:T(4,128)(2,1)}, u32[]{:S(2)}) copy-start(bf16[256,4,128]{2,1,0:T(4,128)(2,1)} %param.8) | copy-start | bytes 786436
  1.7 0.9 %copy-start.1 = (bf16[4,128,128]{2,1,0:T(8,128)(2,1)S(1)}, bf16[4,128,128]{2,1,0:T(8,128)(2,1)}, u32[]{:S(2)}) copy-start(bf16[4,128,128]{2,1,0:T(8,128)(2,1)} %weights_ref.1) | copy-start | bytes 393220
  2.6 1.0 %copy-start.6 = (bf16[768,256]{1,0:T(8,128)(2,1)S(1)}, bf16[768,256]{1,0:T(8,128)(2,1)}, u32[]{:S(2)}) copy-start(bf16[768,256]{1,0:T(8,128)(2,1)} %constant.4.clone.dft_ref) | copy-start | bytes 1179652
  3.6 0.8 %copy-start.7 = (f32[4,9,128]{2,1,0:T(8,128)S(1)}, f32[4,9,128]{2,1,0:T(8,128)}, u32[]{:S(2)}) copy-start(f32[4,9,128]{2,1,0:T(8,128)} %constant.5.clone.turns_ref) | copy-start | bytes 55300

commit v2 on v1

v2 whole, which is shorter than its diff:
```python
import functools
import math

import jax
import jax.numpy as jnp
import numpy as np
from jax import lax
from jax.experimental import pallas as pl
from jax.experimental.pallas import tpu as pltpu
from jax.sharding import PartitionSpec as P

ANG = 2048
TP = 128
Q_DEV = 16
NSEG = 16
HALF = NSEG // 2
FREQS = HALF + 1
ROWS = FREQS * Q_DEV
FIELD = 32
GROUP = 4
BATCH = 8
FIRST = 32
MESH = pl.DeviceIdType.MESH


def dft_tables():
    b = np.arange(TP)
    angle = 2.0 * math.pi * (np.outer(b, b) % TP) / TP
    cos, sin = np.cos(angle), np.sin(angle)
    table = np.block([[cos, -sin], [sin, cos]]).astype(np.float32)
    high = table.astype(jnp.bfloat16)
    low = (table - high.astype(np.float32)).astype(jnp.bfloat16)
    dft = np.concatenate([high, high, low], axis=0)
    twist = 2.0 * math.pi * (np.outer(np.arange(FREQS), b) % ANG) / ANG
    scale = np.full((FREQS, 1), 2.0 / ANG)
    scale[0] = scale[HALF] = 1.0 / ANG
    turns = np.stack(
        [np.cos(twist), -np.sin(twist), scale * np.cos(twist), -scale * np.sin(twist)]
    ).astype(np.float32)
    return dft, turns


def cosine_sums(first, middle, rest):
    c1, c3, r2 = math.cos(math.pi / 8), math.cos(3 * math.pi / 8), math.sqrt(0.5)
    even, odd = first + middle, first - middle
    g, h = rest[2] + rest[6], r2 * (rest[2] - rest[6])
    base = even + rest[4]
    p = [base + g, odd + h, even - rest[4], odd - h, base - g]
    u1, u3 = rest[1] - rest[7], rest[3] - rest[5]
    t1, t3 = rest[1] + rest[7], rest[3] + rest[5]
    q = [t1 + t3, c1 * u1 + c3 * u3, r2 * (t1 - t3), c3 * u1 - c1 * u3]
    low = [p[k] + q[k] for k in range(4)]
    high = [p[k] - q[k] for k in range(3, -1, -1)]
    return low + [p[4]] + high


def sine_sums(v):
    c1, c3, r2 = math.cos(math.pi / 8), math.cos(3 * math.pi / 8), math.sqrt(0.5)
    e = r2 * (v[2] + v[6])
    w = [None, e + v[4], v[2] - v[6], e - v[4]]
    a, b = v[1] + v[7], v[3] + v[5]
    s, t = v[1] - v[7], v[3] - v[5]
    o = [None, c3 * a + c1 * b, r2 * (s + t), c1 * a - c3 * b]
    low = [o[k] + w[k] for k in range(1, 4)]
    high = [o[k] - w[k] for k in range(3, 0, -1)]
    return [None] + low + [s - t] + high


def split(x):
    high = x.astype(jnp.bfloat16)
    return high, (x - high.astype(jnp.float32)).astype(jnp.bfloat16)


def dot(a, b, rhs_dim=0):
    return lax.dot_general(
        a, b, (((1,), (rhs_dim,)), ((), ())), preferred_element_type=jnp.float32
    )


def send_order(owners):
    def hops(i):
        z, y = i // 8, i // 2 % 4
        return min(z, 4 - z) + min(y, 4 - y)

    return [0] + sorted(range(1, owners), key=lambda i: -hops(i))


def layout_tables(owners, cap, tiles):
    order = np.repeat(np.asarray(send_order(owners), np.int32)[:, None], tiles, axis=1)
    j, lane = np.arange(owners * cap)[:, None], np.arange(TP)[None, :]
    source = (j // cap == np.arange(TP)[None, :owners]).astype(jnp.bfloat16)
    entry = ((lane % FIELD == j % cap) & (lane < 3 * FIELD)).astype(np.float32)
    spread = (np.arange(TP)[:, None] // FIELD == np.arange(3 * TP)[None, :] // TP).astype(jnp.bfloat16)
    return order, source, entry, spread


def kernel(
    owners, cap, shots, shot_blocks, operand_count, *refs
):
    hbm, out_ref, rest = refs[:operand_count], refs[operand_count], refs[operand_count + 1 :]
    local, load_sem, rest = rest[:operand_count], rest[operand_count], rest[operand_count + 1 :]
    (
        owner_ref, place_ref, kind_ref, len_ref, order_ref, pix_ref,
        source_ref, entry_ref, spread_ref, weights_ref, turns_ref, dft_ref,
    ) = local
    (
        wide, send, recv, meta, meta_send, meta_recv, fields_col,
        chosen, values, cycles, shares, high, low, spectra, inverse,
        send_sem, first_sem, rest_sem, meta_send_sem, meta_recv_sem, halo_sem,
    ) = rest
    me, block = lax.axis_index("blk"), lax.axis_index("shot")
    tiles = owner_ref.shape[1]
    rows = cap * shots
    halo, mask = shots, shots + 1
    bf16, f32 = jnp.bfloat16, jnp.float32
    left = lax.rem(block + shot_blocks - 1, shot_blocks)
    right = lax.rem(block + 1, shot_blocks)
    order = send_order(owners)

    loads = [
        pltpu.make_async_copy(source, target, load_sem.at[i])
        for i, (source, target) in enumerate(zip(hbm, local))
    ]
    for load in loads:
        load.start()

    barrier = pltpu.get_barrier_semaphore()

    def greet(i, carry):
        pl.semaphore_signal(
            barrier, inc=1, device_id=(block, lax.bitwise_xor(me, i)), device_id_type=MESH
        )
        return carry

    lax.fori_loop(1, owners, greet, 0)
    pl.semaphore_signal(barrier, inc=1, device_id=(right, me), device_id_type=MESH)

    for load in loads[:5]:
        load.wait()

    goes = order_ref[...] == lax.bitwise_xor(owner_ref[...], me)
    goes_bf = goes.astype(f32).astype(bf16)
    before = (
        lax.broadcasted_iota(jnp.int32, (tiles, tiles), 0)
        < lax.broadcasted_iota(jnp.int32, (tiles, tiles), 1)
    ).astype(f32).astype(bf16)
    number = lax.broadcasted_iota(jnp.int32, (owners, tiles), 0).astype(f32)
    earlier = dot(goes_bf, before)
    rank = jnp.sum(jnp.where(goes, earlier, 0.0), axis=0, keepdims=True)
    position = jnp.sum(jnp.where(goes, earlier + number * cap, 0.0), axis=0, keepdims=True)

    place = place_ref[...]
    place = lax.rem(place, NSEG) * Q_DEV + lax.div(place, NSEG)
    at_rank = lax.broadcasted_iota(jnp.int32, (FIELD, tiles), 0).astype(f32) == rank
    fields = [
        jnp.where(at_rank, jnp.broadcast_to(f.astype(f32), at_rank.shape), 0.0)
        for f in (place, kind_ref[...], len_ref[...])
    ]
    fields = jnp.concatenate(fields + [jnp.zeros((FIELD, tiles), f32)], axis=0).astype(bf16)
    meta[...] = dot(goes_bf, fields, 1)

    def lay_meta(i, carry):
        meta_send[i] = meta[pl.ds(i, 1), :]
        return carry

    lax.fori_loop(0, owners, lay_meta, 0)
    meta_recv[0] = meta_send[0]

    loads[5].wait()
    wide[...] = pix_ref[...].astype(f32)
    lengths = len_ref[...].astype(f32)
    lengths = jnp.concatenate(
        [
            jnp.transpose(jnp.broadcast_to(lengths[:, i : i + TP], (TP, TP)))
            for i in range(0, tiles, TP)
        ],
        axis=0,
    )
    live = lax.broadcasted_iota(jnp.int32, (tiles, TP), 1).astype(f32) < lengths
    masked = jnp.concatenate(
        [
            jnp.where(live, wide[pl.ds(s, tiles, stride=shots), :], 0.0).astype(bf16)
            for s in range(shots)
        ],
        axis=1,
    )

    per = 8

    def pack(c, carry):
        spot = lax.broadcasted_iota(jnp.int32, (per * cap, tiles), 0) + c * (per * cap)
        placing = (spot.astype(f32) == position).astype(f32).astype(bf16)
        packed = dot(placing, masked)
        for d in range(per):
            mine = packed[d * cap : (d + 1) * cap]
            mine = jnp.concatenate([mine[:, s * TP : (s + 1) * TP] for s in range(shots)], axis=0)
            send[c * per + d] = mine.astype(bf16)
        return carry

    lax.fori_loop(0, owners // per, pack, 0)
    recv[0] = send[0]

    pl.semaphore_wait(barrier, owners)

    def meta_copy(here, i):
        return pltpu.make_async_remote_copy(
            src_ref=meta_send.at[here], dst_ref=meta_recv.at[here],
            send_sem=meta_send_sem, recv_sem=meta_recv_sem,
            device_id=(block, lax.bitwise_xor(me, i)), device_id_type=MESH,
        )

    def pixel_copy(here, part, sem, i):
        return pltpu.make_async_remote_copy(
            src_ref=send.at[here, part], dst_ref=recv.at[here, part],
            send_sem=send_sem, recv_sem=sem,
            device_id=(block, lax.bitwise_xor(me, i)), device_id_type=MESH,
        )

    first_rows, rest_rows = pl.ds(0, FIRST), pl.ds(FIRST, rows - FIRST)
    for k in range(1, owners):
        meta_copy(k, order[k]).start()
    for k in range(1, owners):
        pixel_copy(k, first_rows, first_sem, order[k]).start()
    for k in range(1, owners):
        pixel_copy(k, rest_rows, rest_sem.at[k // GROUP], order[k]).start()

    others = pl.ds(1, owners - 1)
    for load in loads[6:10]:
        load.wait()
    meta_copy(others, 1).wait_recv()

    entries = dot(source_ref[...], meta_recv[...].reshape(owners, TP).astype(bf16))
    fields_col[...] = dot((entries * entry_ref[...]).astype(bf16), spread_ref[...])
    slots = Q_DEV * NSEG
    slot = lax.broadcasted_iota(jnp.int32, (slots, TP), 0).astype(f32)
    for i in range(owners * cap // TP):
        line = jnp.transpose(fields_col[i * TP : (i + 1) * TP, :TP])
        line = jnp.broadcast_to(line[0:1], (slots, TP))
        chosen[:, i * TP : (i + 1) * TP] = (slot == line).astype(f32).astype(bf16)

    weights = jnp.concatenate([weights_ref[k] for k in range(weights_ref.shape[0])], axis=1)
    kinds = weights_ref.shape[0]

    def pick(kind, product):
        picked = product[:, 0:TP]
        for k in range(1, kinds):
            picked = jnp.where(kind == float(k), product[:, k * TP : (k + 1) * TP], picked)
        return picked

    def keep(here, column, kind, product):
        hi, lo = split(pick(kind, product))
        values[here, 2 * column * TP : (2 * column + 1) * TP] = hi
        values[here, (2 * column + 1) * TP : (2 * column + 2) * TP] = lo

    def interpolate(g, count, start, end, first_shot, last_shot):
        here = pl.ds(pl.multiple_of(g * (count * cap), 16), count * cap)
        kind = fields_col[here, TP : 2 * TP]
        size = end - start
        pixels = recv[pl.ds(g * count, count), start:end].reshape(count * size, TP)
        product = dot(pixels, weights)
        for s in range(first_shot, last_shot):
            mine = [
                product[i * size + s * cap - start : i * size + (s + 1) * cap - start]
                for i in range(count)
            ]
            keep(here, s, kind, jnp.concatenate(mine, axis=0))

    def interpolate_live(g, carry):
        span = BATCH * cap
        here = pl.ds(pl.multiple_of(g * span, 16), span)
        pixel = lax.broadcasted_iota(jnp.int32, (span, TP), 1).astype(f32)
        alive = (pixel < fields_col[here, 2 * TP :]).astype(f32).astype(bf16)
        keep(here, shots, fields_col[here, TP : 2 * TP], dot(alive, weights))
        return carry

    lax.fori_loop(0, owners // BATCH, interpolate_live, 0)

    def gather(s, target):
        both = dot(chosen[...], values[:, 2 * s * TP : (2 * s + 2) * TP])
        cycles[target] = both[:, :TP] + both[:, TP:]

    gather(shots, mask)

    def interpolate_first(g, carry):
        interpolate(g, BATCH, 0, FIRST, 0, 1)
        return carry

    pixel_copy(others, first_rows, first_sem, 1).wait_recv()
    lax.fori_loop(0, owners // BATCH, interpolate_first, 0)
    gather(0, 0)
    halo_copy = pltpu.make_async_remote_copy(
        src_ref=cycles.at[0], dst_ref=cycles.at[halo],
        send_sem=halo_sem.at[0], recv_sem=halo_sem.at[1],
        device_id=(left, me), device_id_type=MESH,
    )
    halo_copy.start()

    def put(here, real, imag):
        for j, part in enumerate((real, imag)):
            hi, lo = split(part)
            high[here, j * TP : (j + 1) * TP] = hi
            low[here, j * TP : (j + 1) * TP] = lo

    def band(s, k):
        return pl.ds(pl.multiple_of(s * ROWS + k * Q_DEV, 16), Q_DEV)

    def forward(s, target):
        x = [cycles[s, a * Q_DEV : (a + 1) * Q_DEV, :] for a in range(NSEG)]
        total = [None] + [x[a] + x[NSEG - a] for a in range(1, HALF)]
        differ = [None] + [x[a] - x[NSEG - a] for a in range(1, HALF)]
        real = cosine_sums(x[0], x[HALF], total)
        imag = sine_sums(differ)
        for k in range(FREQS):
            here = band(target, k)
            cos, sin = turns_ref[0, k : k + 1, :], turns_ref[1, k : k + 1, :]
            if k == 0:
                put(here, real[k], jnp.zeros_like(real[k]))
            elif k == HALF:
                put(here, real[k] * cos, real[k] * sin)
            else:
                put(here, real[k] * cos + imag[k] * sin, real[k] * sin - imag[k] * cos)

    def transform(first, count):
        here = pl.ds(first * ROWS, count * ROWS)
        hi, lo = high[here, :], low[here, :]
        return dot(jnp.concatenate([hi, lo, hi], axis=1), dft_ref[...])

    def correlate(s, following, target):
        for k in range(FREQS):
            mine = spectra[band(s, k), :]
            xr, xi = mine[:, :TP], mine[:, TP:]
            if following is None:
                put(band(target, k), xr * xr + xi * xi, jnp.zeros_like(xr))
            else:
                differ = mine - spectra[band(following, k), :]
                dr, di = differ[:, :TP], differ[:, TP:]
                put(band(target, k), xr * dr + xi * di, xr * di - xi * dr)

    def back(s):
        parts = []
        for k in range(FREQS):
            here = band(s, k)
            re, im = inverse[here, :TP], inverse[here, TP:]
            cos, sin = turns_ref[2, k : k + 1, :], turns_ref[3, k : k + 1, :]
            parts.append((re * cos - im * sin, re * sin + im * cos))
        sums = cosine_sums(parts[0][0], parts[HALF][0], [p[0] for p in parts])
        turned = sine_sums([p[1] for p in parts])
        found = [None] * NSEG
        found[0], found[HALF] = sums[0], sums[HALF]
        for a in range(1, HALF):
            found[a], found[NSEG - a] = sums[a] + turned[a], sums[a] - turned[a]
        return found

    for load in loads[10:]:
        load.wait()
    forward(0, 0)
    forward(mask, 1)
    spectra[0 : 2 * ROWS, :] = transform(0, 2)
    correlate(1, None, 0)
    inverse[0:ROWS, :] = transform(0, 1)
    overlap = back(0)
    floor = jnp.maximum(0.01 * overlap[0][:, 0:1], 1.0)
    for a in range(NSEG):
        shares[a * Q_DEV : (a + 1) * Q_DEV, :] = 1.0 / jnp.maximum(overlap[a], floor)

    def receive(first, count, g):
        pixel_copy(pl.ds(first, count), rest_rows, rest_sem.at[g], 1).wait_recv()

    receive(1, GROUP - 1, 0)
    interpolate(0, GROUP, 16, rows, 1, shots)

    def take_group(g, carry):
        receive(g * GROUP, GROUP, g)
        interpolate(g, GROUP, 16, rows, 1, shots)
        return carry

    lax.fori_loop(1, owners // GROUP, take_group, 0)
    for s in range(1, shots):
        gather(s, s)
    halo_copy.wait_recv()

    def forward_shot(s, carry):
        forward(s, s)
        return carry

    lax.fori_loop(1, shots + 1, forward_shot, 0)
    spectra[ROWS : (shots + 1) * ROWS, :] = transform(1, shots)

    def correlate_shot(s, carry):
        correlate(s, s + 1, s)
        return carry

    lax.fori_loop(0, shots, correlate_shot, 0)
    inverse[0 : shots * ROWS, :] = transform(0, shots)

    def finish_shot(s, carry):
        found = back(s)
        for a in range(NSEG):
            share = shares[a * Q_DEV : (a + 1) * Q_DEV, :]
            out_ref[s, :, a * TP : (a + 1) * TP] = found[a] * share
        return carry

    lax.fori_loop(0, shots, finish_shot, 0)

    halo_copy.wait_send()
    meta_copy(others, 1).wait_send()
    pixel_copy(others, pl.ds(0, rows), first_sem, 1).wait_send()


def per_device(intensities, tile_owner, tile_place, tile_kernel, mask_len, interp_weights):
    owners, shot_blocks = lax.axis_size("blk"), lax.axis_size("shot")
    tiles, shots, _ = intensities.shape
    cap = 3 * tiles // owners
    dft, turns = dft_tables()
    order, source, entry, spread = layout_tables(owners, cap, tiles)
    bf16, f32 = jnp.bfloat16, jnp.float32
    slots = Q_DEV * NSEG
    operands = (
        tile_owner.reshape(1, tiles),
        tile_place.reshape(1, tiles),
        tile_kernel.reshape(1, tiles),
        mask_len.reshape(1, tiles),
        jnp.asarray(order),
        intensities.reshape(tiles * shots, TP),
        jnp.asarray(source),
        jnp.asarray(entry),
        jnp.asarray(spread),
        interp_weights,
        jnp.asarray(turns),
        jnp.asarray(dft),
    )
    return pl.pallas_call(
        functools.partial(kernel, owners, cap, shots, shot_blocks, len(operands)),
        out_shape=jax.ShapeDtypeStruct((shots, Q_DEV, ANG), f32),
        in_specs=[pl.BlockSpec(memory_space=pltpu.HBM)] * len(operands),
        out_specs=pl.BlockSpec(memory_space=pltpu.VMEM),
        scratch_shapes=[pltpu.VMEM(x.shape, x.dtype) for x in operands]
        + [pltpu.SemaphoreType.DMA((len(operands),))]
        + [
            pltpu.VMEM((tiles * shots, TP), f32),
            pltpu.VMEM((owners, cap * shots, TP), bf16),
            pltpu.VMEM((owners, cap * shots, TP), bf16),
            pltpu.VMEM((owners, TP), f32),
            pltpu.VMEM((owners, 1, TP), f32),
            pltpu.VMEM((owners, 1, TP), f32),
            pltpu.VMEM((owners * cap, 3 * TP), f32),
            pltpu.VMEM((slots, owners * cap), bf16),
            pltpu.VMEM((owners * cap, (shots + 1) * 2 * TP), bf16),
            pltpu.VMEM((shots + 2, slots, TP), f32),
            pltpu.VMEM((slots, TP), f32),
            pltpu.VMEM(((shots + 1) * ROWS, 2 * TP), bf16),
            pltpu.VMEM(((shots + 1) * ROWS, 2 * TP), bf16),
            pltpu.VMEM(((shots + 1) * ROWS, 2 * TP), f32),
            pltpu.VMEM((shots * ROWS, 2 * TP), f32),
            pltpu.SemaphoreType.DMA,
            pltpu.SemaphoreType.DMA,
            pltpu.SemaphoreType.DMA((owners // GROUP,)),
            pltpu.SemaphoreType.DMA,
            pltpu.SemaphoreType.DMA,
            pltpu.SemaphoreType.DMA((2,)),
        ],
        compiler_params=pltpu.CompilerParams(
            collective_id=0, has_side_effects=True, vmem_limit_bytes=40 * 2**20
        ),
        cost_estimate=pl.CostEstimate(
            flops=3 * 10**9, bytes_accessed=2 * 10**6, transcendentals=0
        ),
    )(*(pltpu.with_memory_space_constraint(x, pltpu.HBM) for x in operands))


def solution(mesh):
    placed = (P("blk", "shot", None), P("blk"), P("blk"), P("blk"), P("blk"), P())
    return jax.shard_map(
        per_device, mesh=mesh, in_specs=placed, out_specs=P("shot", "blk", None), check_vma=False
    )
```

time: 32.9 us -> 23.8 us (0.72)
  the two profiles are of different devices: /device:TPU:10 before, /device:TPU:1 now
where the time goes in v2:
time: 23.8 us; the launch traced here: 23.7 us
  Pallas kernels  22.9 us (96%)
  local copies, waits for them, and re-layouts  0.8 us (3%)
    pallas_call x1, Pallas kernels, per_device(): pl.pallas_call(functools.partial(kernel, owners, cap, shots, shot_blocks,...  22.9 us
    unnamed x1, local copies, waits for them, and re-layouts  0.8 us

profile of v2, /device:TPU:1, one launch (start us, length us, event | category | flops | bytes accessed | tf_op | source)
XLA Modules:
  0.0 23.7 jit_solution(15302141113144099041)
XLA Ops:
  0.0 22.9 %shard_map.118 = f32[4,16,2048]{2,1,0:T(8,128)S(1)} custom-call(s32[1,256]{1,0:T(1,128)} %bitcast.6, s32[1,256]{1,0:T(1,128)} %bitcast.7, s32[1,256]{1,0:T(1,128)} %bitcast.8, s32[1,256]{1,0:T(1,128)} %bitcast.9, s32[32,256]{1,0:T(8,128)} %constant.12.clone.refs_4_, bf16[1024,128]{1,0:T(8,128)(2,1)} %bitcast.5, bf16[768,32]{1,0:T(8,128)(2,1)} %constant.13.clone.refs_6_, ...), custom_call_target="tpu_custom_call" | custom-call | flops 3000000000 | bytes 2000000 | tf_op jit(solution)/shard_map/pallas_call | solution.py:432
  22.9 0.8 %copy.14 = f32[4,16,2048]{2,1,0:T(8,128)} copy(f32[4,16,2048]{2,1,0:T(8,128)S(1)} %shard_map.118) | data formatting | bytes 1048576

commit v3 on v2

--- a/solution.py
+++ b/solution.py
@@ -17,9 +17,9 @@
 FREQS = HALF + 1
 ROWS = FREQS * Q_DEV
 FIELD = 32
-GROUP = 4
-BATCH = 8
-FIRST = 32
+STARTS = (0, 16, 32)
+BATCH = 16
+LATE = 1
 MESH = pl.DeviceIdType.MESH
 
 
@@ -105,17 +105,28 @@
     ) = local
     (
         wide, send, recv, meta, meta_send, meta_recv, fields_col,
-        chosen, values, cycles, shares, high, low, spectra, inverse,
-        send_sem, first_sem, rest_sem, meta_send_sem, meta_recv_sem, halo_sem,
+        is_kind, chosen, values, cycles, shares, high, low, spectra, inverse,
+        send_sem, piece_sem, meta_send_sem, meta_recv_sem, halo_sem,
     ) = rest
     me, block = lax.axis_index("blk"), lax.axis_index("shot")
     tiles = owner_ref.shape[1]
     rows = cap * shots
     halo, mask = shots, shots + 1
+    turned_back = shots + 2
     bf16, f32 = jnp.bfloat16, jnp.float32
     left = lax.rem(block + shot_blocks - 1, shot_blocks)
     right = lax.rem(block + 1, shot_blocks)
     order = send_order(owners)
+
+    barrier = pltpu.get_barrier_semaphore()
+    pl.semaphore_signal(barrier, inc=1, device_id=(right, me), device_id_type=MESH)
+    for k in range(1, owners):
+        pl.semaphore_signal(
+            barrier,
+            inc=1,
+            device_id=(block, lax.bitwise_xor(me, order[k])),
+            device_id_type=MESH,
+        )
 
     loads = [
         pltpu.make_async_copy(source, target, load_sem.at[i])
@@ -123,17 +134,6 @@
     ]
     for load in loads:
         load.start()
-
-    barrier = pltpu.get_barrier_semaphore()
-
-    def greet(i, carry):
-        pl.semaphore_signal(
-            barrier, inc=1, device_id=(block, lax.bitwise_xor(me, i)), device_id_type=MESH
-        )
-        return carry
-
-    lax.fori_loop(1, owners, greet, 0)
-    pl.semaphore_signal(barrier, inc=1, device_id=(right, me), device_id_type=MESH)
 
     for load in loads[:5]:
         load.wait()
@@ -185,23 +185,6 @@
         axis=1,
     )
 
-    per = 8
-
-    def pack(c, carry):
-        spot = lax.broadcasted_iota(jnp.int32, (per * cap, tiles), 0) + c * (per * cap)
-        placing = (spot.astype(f32) == position).astype(f32).astype(bf16)
-        packed = dot(placing, masked)
-        for d in range(per):
-            mine = packed[d * cap : (d + 1) * cap]
-            mine = jnp.concatenate([mine[:, s * TP : (s + 1) * TP] for s in range(shots)], axis=0)
-            send[c * per + d] = mine.astype(bf16)
-        return carry
-
-    lax.fori_loop(0, owners // per, pack, 0)
-    recv[0] = send[0]
-
-    pl.semaphore_wait(barrier, owners)
-
     def meta_copy(here, i):
         return pltpu.make_async_remote_copy(
             src_ref=meta_send.at[here], dst_ref=meta_recv.at[here],
@@ -216,13 +199,33 @@
             device_id=(block, lax.bitwise_xor(me, i)), device_id_type=MESH,
         )
 
-    first_rows, rest_rows = pl.ds(0, FIRST), pl.ds(FIRST, rows - FIRST)
+    def group_of(k):
+        return sum(k >= start for start in STARTS[1:-1])
+
+    third = rows // 3
+    pieces = [pl.ds(part * third, third) for part in range(3)]
+
+    def pack(first, count):
+        spot = lax.broadcasted_iota(jnp.int32, (count * cap, tiles), 0) + first * cap
+        placing = (spot.astype(f32) == position).astype(f32).astype(bf16)
+        packed = dot(placing, masked)
+        for d in range(count):
+            mine = packed[d * cap : (d + 1) * cap]
+            mine = jnp.concatenate([mine[:, s * TP : (s + 1) * TP] for s in range(shots)], axis=0)
+            send[first + d] = mine.astype(bf16)
+
+    for first in range(0, owners, BATCH):
+        pack(first, BATCH)
+    recv[0] = send[0]
+
+    pl.semaphore_wait(barrier, owners)
     for k in range(1, owners):
         meta_copy(k, order[k]).start()
+    for part in range(2):
+        for k in range(1, owners):
+            pixel_copy(k, pieces[part], piece_sem.at[part], order[k]).start()
     for k in range(1, owners):
-        pixel_copy(k, first_rows, first_sem, order[k]).start()
-    for k in range(1, owners):
-        pixel_copy(k, rest_rows, rest_sem.at[k // GROUP], order[k]).start()
+        pixel_copy(k, pieces[2], piece_sem.at[2 + group_of(k)], order[k]).start()
 
     others = pl.ds(1, owners - 1)
     for load in loads[6:10]:
@@ -238,62 +241,55 @@
         line = jnp.broadcast_to(line[0:1], (slots, TP))
         chosen[:, i * TP : (i + 1) * TP] = (slot == line).astype(f32).astype(bf16)
 
-    weights = jnp.concatenate([weights_ref[k] for k in range(weights_ref.shape[0])], axis=1)
     kinds = weights_ref.shape[0]
-
-    def pick(kind, product):
-        picked = product[:, 0:TP]
-        for k in range(1, kinds):
-            picked = jnp.where(kind == float(k), product[:, k * TP : (k + 1) * TP], picked)
-        return picked
-
-    def keep(here, column, kind, product):
-        hi, lo = split(pick(kind, product))
+    weights = weights_ref[...].reshape(kinds * TP, TP)
+
+    def mark_kinds(i, carry):
+        kind = fields_col[pl.ds(pl.multiple_of(i * cap, 8), cap), TP : 2 * TP]
+        for k in range(kinds):
+            one = (kind == float(k)).astype(f32)
+            is_kind[k, i] = jnp.concatenate([one] * shots, axis=0).astype(bf16)
+        return carry
+
+    def keep(here, column, product):
+        hi, lo = split(product)
         values[here, 2 * column * TP : (2 * column + 1) * TP] = hi
         values[here, (2 * column + 1) * TP : (2 * column + 2) * TP] = lo
 
-    def interpolate(g, count, start, end, first_shot, last_shot):
-        here = pl.ds(pl.multiple_of(g * (count * cap), 16), count * cap)
-        kind = fields_col[here, TP : 2 * TP]
-        size = end - start
-        pixels = recv[pl.ds(g * count, count), start:end].reshape(count * size, TP)
-        product = dot(pixels, weights)
+    def interpolate(first, count, start, end, first_shot, last_shot):
+        here = pl.ds(pl.multiple_of(first * cap, 16), count * cap)
+        size, these = end - start, pl.ds(first, count)
+        pixels = recv[these, start:end].reshape(count * size, TP)
+        spread = [
+            pixels * is_kind[k, these, start:end].reshape(count * size, TP) for k in range(kinds)
+        ]
+        product = dot(jnp.concatenate(spread, axis=1), weights)
         for s in range(first_shot, last_shot):
             mine = [
                 product[i * size + s * cap - start : i * size + (s + 1) * cap - start]
                 for i in range(count)
             ]
-            keep(here, s, kind, jnp.concatenate(mine, axis=0))
+            keep(here, s, jnp.concatenate(mine, axis=0))
 
     def interpolate_live(g, carry):
         span = BATCH * cap
         here = pl.ds(pl.multiple_of(g * span, 16), span)
         pixel = lax.broadcasted_iota(jnp.int32, (span, TP), 1).astype(f32)
-        alive = (pixel < fields_col[here, 2 * TP :]).astype(f32).astype(bf16)
-        keep(here, shots, fields_col[here, TP : 2 * TP], dot(alive, weights))
+        kind = fields_col[here, TP : 2 * TP]
+        alive = jnp.where(pixel < fields_col[here, 2 * TP :], kind, -1.0)
+        spread = [(alive == float(k)).astype(f32).astype(bf16) for k in range(kinds)]
+        keep(here, shots, dot(jnp.concatenate(spread, axis=1), weights))
         return carry
 
     lax.fori_loop(0, owners // BATCH, interpolate_live, 0)
-
-    def gather(s, target):
-        both = dot(chosen[...], values[:, 2 * s * TP : (2 * s + 2) * TP])
-        cycles[target] = both[:, :TP] + both[:, TP:]
+    lax.fori_loop(0, owners, mark_kinds, 0)
+
+    def gather(s, target, start=0, end=owners * cap):
+        both = dot(chosen[:, start:end], values[start:end, 2 * s * TP : (2 * s + 2) * TP])
+        both = both[:, :TP] + both[:, TP:]
+        cycles[target] = both + cycles[target] if start else both
 
     gather(shots, mask)
-
-    def interpolate_first(g, carry):
-        interpolate(g, BATCH, 0, FIRST, 0, 1)
-        return carry
-
-    pixel_copy(others, first_rows, first_sem, 1).wait_recv()
-    lax.fori_loop(0, owners // BATCH, interpolate_first, 0)
-    gather(0, 0)
-    halo_copy = pltpu.make_async_remote_copy(
-        src_ref=cycles.at[0], dst_ref=cycles.at[halo],
-        send_sem=halo_sem.at[0], recv_sem=halo_sem.at[1],
-        device_id=(left, me), device_id_type=MESH,
-    )
-    halo_copy.start()
 
     def put(here, real, imag):
         for j, part in enumerate((real, imag)):
@@ -304,14 +300,14 @@
     def band(s, k):
         return pl.ds(pl.multiple_of(s * ROWS + k * Q_DEV, 16), Q_DEV)
 
-    def forward(s, target):
+    def forward(s):
         x = [cycles[s, a * Q_DEV : (a + 1) * Q_DEV, :] for a in range(NSEG)]
         total = [None] + [x[a] + x[NSEG - a] for a in range(1, HALF)]
         differ = [None] + [x[a] - x[NSEG - a] for a in range(1, HALF)]
         real = cosine_sums(x[0], x[HALF], total)
         imag = sine_sums(differ)
         for k in range(FREQS):
-            here = band(target, k)
+            here = band(s, k)
             cos, sin = turns_ref[0, k : k + 1, :], turns_ref[1, k : k + 1, :]
             if k == 0:
                 put(here, real[k], jnp.zeros_like(real[k]))
@@ -320,10 +316,11 @@
             else:
                 put(here, real[k] * cos + imag[k] * sin, real[k] * sin - imag[k] * cos)
 
-    def transform(first, count):
+    def transform(result, target, first, count):
         here = pl.ds(first * ROWS, count * ROWS)
         hi, lo = high[here, :], low[here, :]
-        return dot(jnp.concatenate([hi, lo, hi], axis=1), dft_ref[...])
+        found = dot(jnp.concatenate([hi, lo, hi], axis=1), dft_ref[...])
+        result[pl.ds(target * ROWS, count * ROWS), :] = found
 
     def correlate(s, following, target):
         for k in range(FREQS):
@@ -353,58 +350,77 @@
 
     for load in loads[10:]:
         load.wait()
-    forward(0, 0)
-    forward(mask, 1)
-    spectra[0 : 2 * ROWS, :] = transform(0, 2)
-    correlate(1, None, 0)
-    inverse[0:ROWS, :] = transform(0, 1)
-    overlap = back(0)
+    forward(mask)
+    transform(spectra, mask, mask, 1)
+    correlate(mask, None, turned_back + shots)
+    transform(inverse, shots, turned_back + shots, 1)
+    overlap = back(shots)
     floor = jnp.maximum(0.01 * overlap[0][:, 0:1], 1.0)
     for a in range(NSEG):
         shares[a * Q_DEV : (a + 1) * Q_DEV, :] = 1.0 / jnp.maximum(overlap[a], floor)
 
-    def receive(first, count, g):
-        pixel_copy(pl.ds(first, count), rest_rows, rest_sem.at[g], 1).wait_recv()
-
-    receive(1, GROUP - 1, 0)
-    interpolate(0, GROUP, 16, rows, 1, shots)
-
-    def take_group(g, carry):
-        receive(g * GROUP, GROUP, g)
-        interpolate(g, GROUP, 16, rows, 1, shots)
-        return carry
-
-    lax.fori_loop(1, owners // GROUP, take_group, 0)
-    for s in range(1, shots):
-        gather(s, s)
-    halo_copy.wait_recv()
-
-    def forward_shot(s, carry):
-        forward(s, s)
-        return carry
-
-    lax.fori_loop(1, shots + 1, forward_shot, 0)
-    spectra[ROWS : (shots + 1) * ROWS, :] = transform(1, shots)
-
-    def correlate_shot(s, carry):
-        correlate(s, s + 1, s)
-        return carry
-
-    lax.fori_loop(0, shots, correlate_shot, 0)
-    inverse[0 : shots * ROWS, :] = transform(0, shots)
-
-    def finish_shot(s, carry):
+    def finish(s):
         found = back(s)
         for a in range(NSEG):
             share = shares[a * Q_DEV : (a + 1) * Q_DEV, :]
             out_ref[s, :, a * TP : (a + 1) * TP] = found[a] * share
-        return carry
-
-    lax.fori_loop(0, shots, finish_shot, 0)
+
+    pixel_copy(others, pieces[0], piece_sem.at[0], 1).wait_recv()
+    for first in range(0, owners, BATCH):
+        interpolate(first, BATCH, 0, third, 0, 1)
+    gather(0, 0)
+    halo_copy = pltpu.make_async_remote_copy(
+        src_ref=cycles.at[0], dst_ref=cycles.at[halo],
+        send_sem=halo_sem.at[0], recv_sem=halo_sem.at[1],
+        device_id=(left, me), device_id_type=MESH,
+    )
+    halo_copy.start()
+    forward(0)
+    transform(spectra, 0, 0, 1)
+
+    pixel_copy(others, pieces[1], piece_sem.at[1], 1).wait_recv()
+    for first in range(0, owners, BATCH):
+        interpolate(first, BATCH, 16, 48, 1, 2)
+    gather(1, 1)
+    forward(1)
+    transform(spectra, 1, 1, 1)
+    correlate(0, 1, turned_back)
+    transform(inverse, 0, turned_back, 1)
+    finish(0)
+
+    def take_group(g):
+        skip = 1 if g == 0 else 0
+        pixel_copy(
+            pl.ds(STARTS[g] + skip, STARTS[g + 1] - STARTS[g] - skip),
+            pieces[2],
+            piece_sem.at[2 + g],
+            1,
+        ).wait_recv()
+        interpolate(STARTS[g], STARTS[g + 1] - STARTS[g], 48, rows, 2, shots)
+
+    groups = len(STARTS) - 1
+    early = STARTS[groups - LATE] * cap
+    for g in range(groups - LATE):
+        take_group(g)
+    for s in range(2, shots):
+        gather(s, s, 0, early)
+    for g in range(groups - LATE, groups):
+        take_group(g)
+    for s in range(2, shots):
+        gather(s, s, early, owners * cap)
+        forward(s)
+    halo_copy.wait_recv()
+    forward(halo)
+    transform(spectra, 2, 2, shots - 1)
+    for s in range(1, shots):
+        correlate(s, s + 1, turned_back + s)
+    transform(inverse, 1, turned_back + 1, shots - 1)
+    for s in range(1, shots):
+        finish(s)
 
     halo_copy.wait_send()
     meta_copy(others, 1).wait_send()
-    pixel_copy(others, pl.ds(0, rows), first_sem, 1).wait_send()
+    pixel_copy(others, pl.ds(0, rows), piece_sem.at[0], 1).wait_send()
 
 
 def per_device(intensities, tile_owner, tile_place, tile_kernel, mask_len, interp_weights):
@@ -444,17 +460,17 @@
             pltpu.VMEM((owners, 1, TP), f32),
             pltpu.VMEM((owners, 1, TP), f32),
             pltpu.VMEM((owners * cap, 3 * TP), f32),
+            pltpu.VMEM((interp_weights.shape[0], owners, cap * shots, TP), bf16),
             pltpu.VMEM((slots, owners * cap), bf16),
             pltpu.VMEM((owners * cap, (shots + 1) * 2 * TP), bf16),
             pltpu.VMEM((shots + 2, slots, TP), f32),
             pltpu.VMEM((slots, TP), f32),
-            pltpu.VMEM(((shots + 1) * ROWS, 2 * TP), bf16),
-            pltpu.VMEM(((shots + 1) * ROWS, 2 * TP), bf16),
+            pltpu.VMEM(((2 * shots + 3) * ROWS, 2 * TP), bf16),
+            pltpu.VMEM(((2 * shots + 3) * ROWS, 2 * TP), bf16),
+            pltpu.VMEM(((shots + 2) * ROWS, 2 * TP), f32),
             pltpu.VMEM(((shots + 1) * ROWS, 2 * TP), f32),
-            pltpu.VMEM((shots * ROWS, 2 * TP), f32),
             pltpu.SemaphoreType.DMA,
-            pltpu.SemaphoreType.DMA,
-            pltpu.SemaphoreType.DMA((owners // GROUP,)),
+            pltpu.SemaphoreType.DMA((len(STARTS) + 1,)),
             pltpu.SemaphoreType.DMA,
             pltpu.SemaphoreType.DMA,
             pltpu.SemaphoreType.DMA((2,)),

time: 23.8 us -> 22.7 us (0.954)
  Pallas kernels: 22.9 us -> 21.8 us
    pallas_call x1, Pallas kernels: 22.9 us -> 21.8 us  [per_device(): pl.pallas_call(functools.partial(kernel, owners, cap, shots, shot_blocks,...]
where the time goes in v3:
time: 22.7 us; the launch traced here: 22.6 us
  Pallas kernels  21.8 us (96%)
  local copies, waits for them, and re-layouts  0.8 us (4%)
    pallas_call x1, Pallas kernels, per_device(): pl.pallas_call(functools.partial(kernel, owners, cap, shots, shot_blocks,...  21.8 us
    unnamed x1, local copies, waits for them, and re-layouts  0.8 us

profile of v3, /device:TPU:1, one launch (start us, length us, event | category | flops | bytes accessed | tf_op | source)
XLA Modules:
  0.0 22.6 jit_solution(14716099014199494631)
XLA Ops:
  0.0 21.8 %shard_map.118 = f32[4,16,2048]{2,1,0:T(8,128)S(1)} custom-call(s32[1,256]{1,0:T(1,128)} %bitcast.6, s32[1,256]{1,0:T(1,128)} %bitcast.7, s32[1,256]{1,0:T(1,128)} %bitcast.8, s32[1,256]{1,0:T(1,128)} %bitcast.9, s32[32,256]{1,0:T(8,128)} %constant.12.clone.refs_4_, bf16[1024,128]{1,0:T(8,128)(2,1)} %bitcast.5, bf16[768,32]{1,0:T(8,128)(2,1)} %constant.13.clone.refs_6_, ...), custom_call_target="tpu_custom_call" | custom-call | flops 3000000000 | bytes 2000000 | tf_op jit(solution)/shard_map/pallas_call | solution.py:448
  21.8 0.8 %copy.14 = f32[4,16,2048]{2,1,0:T(8,128)} copy(f32[4,16,2048]{2,1,0:T(8,128)S(1)} %shard_map.118) | data formatting | bytes 1048576

commit v4 on v3

--- a/solution.py
+++ b/solution.py
@@ -246,9 +246,7 @@
 
     def mark_kinds(i, carry):
         kind = fields_col[pl.ds(pl.multiple_of(i * cap, 8), cap), TP : 2 * TP]
-        for k in range(kinds):
-            one = (kind == float(k)).astype(f32)
-            is_kind[k, i] = jnp.concatenate([one] * shots, axis=0).astype(bf16)
+        is_kind[i] = jnp.concatenate([kind] * shots, axis=0).astype(bf16)
         return carry
 
     def keep(here, column, product):
@@ -260,9 +258,9 @@
         here = pl.ds(pl.multiple_of(first * cap, 16), count * cap)
         size, these = end - start, pl.ds(first, count)
         pixels = recv[these, start:end].reshape(count * size, TP)
-        spread = [
-            pixels * is_kind[k, these, start:end].reshape(count * size, TP) for k in range(kinds)
-        ]
+        kind = is_kind[these, start:end].reshape(count * size, TP)
+        none = jnp.zeros_like(pixels)
+        spread = [jnp.where(kind == jnp.asarray(k, bf16), pixels, none) for k in range(kinds)]
         product = dot(jnp.concatenate(spread, axis=1), weights)
         for s in range(first_shot, last_shot):
             mine = [
@@ -411,10 +409,11 @@
         forward(s)
     halo_copy.wait_recv()
     forward(halo)
-    transform(spectra, 2, 2, shots - 1)
+    for s in range(2, shots + 1):
+        transform(spectra, s, s, 1)
     for s in range(1, shots):
         correlate(s, s + 1, turned_back + s)
-    transform(inverse, 1, turned_back + 1, shots - 1)
+        transform(inverse, s, turned_back + s, 1)
     for s in range(1, shots):
         finish(s)
 
@@ -460,7 +459,7 @@
             pltpu.VMEM((owners, 1, TP), f32),
             pltpu.VMEM((owners, 1, TP), f32),
             pltpu.VMEM((owners * cap, 3 * TP), f32),
-            pltpu.VMEM((interp_weights.shape[0], owners, cap * shots, TP), bf16),
+            pltpu.VMEM((owners, cap * shots, TP), bf16),
             pltpu.VMEM((slots, owners * cap), bf16),
             pltpu.VMEM((owners * cap, (shots + 1) * 2 * TP), bf16),
             pltpu.VMEM((shots + 2, slots, TP), f32),

time: 22.7 us -> 22.6 us (level)
  no operation moved by 1% of the time
where the time goes in v4:
time: 22.6 us; the launch traced here: 22.4 us
  Pallas kernels  21.6 us (96%)
  local copies, waits for them, and re-layouts  0.8 us (4%)
    pallas_call x1, Pallas kernels, per_device(): pl.pallas_call(functools.partial(kernel, owners, cap, shots, shot_blocks,...  21.6 us
    unnamed x1, local copies, waits for them, and re-layouts  0.8 us

profile of v4, /device:TPU:1, one launch (start us, length us, event | category | flops | bytes accessed | tf_op | source)
XLA Modules:
  0.0 22.4 jit_solution(4932042175856923185)
XLA Ops:
  0.0 21.6 %shard_map.118 = f32[4,16,2048]{2,1,0:T(8,128)S(1)} custom-call(s32[1,256]{1,0:T(1,128)} %bitcast.6, s32[1,256]{1,0:T(1,128)} %bitcast.7, s32[1,256]{1,0:T(1,128)} %bitcast.8, s32[1,256]{1,0:T(1,128)} %bitcast.9, s32[32,256]{1,0:T(8,128)} %constant.12.clone.refs_4_, bf16[1024,128]{1,0:T(8,128)(2,1)} %bitcast.5, bf16[768,32]{1,0:T(8,128)(2,1)} %constant.13.clone.refs_6_, ...), custom_call_target="tpu_custom_call" | custom-call | flops 3000000000 | bytes 2000000 | tf_op jit(solution)/shard_map/pallas_call | solution.py:447
  21.6 0.8 %copy.14 = f32[4,16,2048]{2,1,0:T(8,128)} copy(f32[4,16,2048]{2,1,0:T(8,128)S(1)} %shard_map.118) | data formatting | bytes 1048576

commit v5 on v4

--- a/solution.py
+++ b/solution.py
@@ -167,7 +167,7 @@
     meta_recv[0] = meta_send[0]
 
     loads[5].wait()
-    wide[...] = pix_ref[...].astype(f32)
+    wide[0 : tiles * shots, :] = pix_ref[...].astype(f32)
     lengths = len_ref[...].astype(f32)
     lengths = jnp.concatenate(
         [
@@ -452,7 +452,7 @@
         scratch_shapes=[pltpu.VMEM(x.shape, x.dtype) for x in operands]
         + [pltpu.SemaphoreType.DMA((len(operands),))]
         + [
-            pltpu.VMEM((tiles * shots, TP), f32),
+            pltpu.VMEM(((tiles + Q_DEV) * shots, TP), f32),
             pltpu.VMEM((owners, cap * shots, TP), bf16),
             pltpu.VMEM((owners, cap * shots, TP), bf16),
             pltpu.VMEM((owners, TP), f32),

time: 22.6 us -> 22.6 us (level)
  no operation moved by 1% of the time
where the time goes in v5:
time: 22.6 us; the launch traced here: 22.4 us
  Pallas kernels  21.6 us (96%)
  local copies, waits for them, and re-layouts  0.8 us (4%)
    pallas_call x1, Pallas kernels, per_device(): pl.pallas_call(functools.partial(kernel, owners, cap, shots, shot_blocks,...  21.6 us
    unnamed x1, local copies, waits for them, and re-layouts  0.8 us

profile of v5, /device:TPU:1, one launch (start us, length us, event | category | flops | bytes accessed | tf_op | source)
XLA Modules:
  0.0 22.4 jit_solution(811174848788489010)
XLA Ops:
  0.0 21.6 %shard_map.118 = f32[4,16,2048]{2,1,0:T(8,128)S(1)} custom-call(s32[1,256]{1,0:T(1,128)} %bitcast.6, s32[1,256]{1,0:T(1,128)} %bitcast.7, s32[1,256]{1,0:T(1,128)} %bitcast.8, s32[1,256]{1,0:T(1,128)} %bitcast.9, s32[32,256]{1,0:T(8,128)} %constant.12.clone.refs_4_, bf16[1024,128]{1,0:T(8,128)(2,1)} %bitcast.5, bf16[768,32]{1,0:T(8,128)(2,1)} %constant.13.clone.refs_6_, ...), custom_call_target="tpu_custom_call" | custom-call | flops 3000000000 | bytes 2000000 | tf_op jit(solution)/shard_map/pallas_call | solution.py:447
  21.6 0.8 %copy.14 = f32[4,16,2048]{2,1,0:T(8,128)} copy(f32[4,16,2048]{2,1,0:T(8,128)S(1)} %shard_map.118) | data formatting | bytes 1048576

commit v6 on v4

--- a/solution.py
+++ b/solution.py
@@ -224,13 +224,14 @@
     for part in range(2):
         for k in range(1, owners):
             pixel_copy(k, pieces[part], piece_sem.at[part], order[k]).start()
-    for k in range(1, owners):
-        pixel_copy(k, pieces[2], piece_sem.at[2 + group_of(k)], order[k]).start()
 
     others = pl.ds(1, owners - 1)
     for load in loads[6:10]:
         load.wait()
     meta_copy(others, 1).wait_recv()
+
+    for k in range(1, owners):
+        pixel_copy(k, pieces[2], piece_sem.at[2 + group_of(k)], order[k]).start()
 
     entries = dot(source_ref[...], meta_recv[...].reshape(owners, TP).astype(bf16))
     fields_col[...] = dot((entries * entry_ref[...]).astype(bf16), spread_ref[...])

time: 22.6 us -> 22.6 us (level)
  no operation moved by 1% of the time
where the time goes in v6:
time: 22.6 us; the launch traced here: 22.4 us
  Pallas kernels  21.6 us (96%)
  local copies, waits for them, and re-layouts  0.8 us (4%)
    pallas_call x1, Pallas kernels, per_device(): pl.pallas_call(functools.partial(kernel, owners, cap, shots, shot_blocks,...  21.6 us
    unnamed x1, local copies, waits for them, and re-layouts  0.8 us

profile of v6, /device:TPU:1, one launch (start us, length us, event | category | flops | bytes accessed | tf_op | source)
XLA Modules:
  0.0 22.4 jit_solution(13003394289927378954)
XLA Ops:
  0.0 21.6 %shard_map.118 = f32[4,16,2048]{2,1,0:T(8,128)S(1)} custom-call(s32[1,256]{1,0:T(1,128)} %bitcast.6, s32[1,256]{1,0:T(1,128)} %bitcast.7, s32[1,256]{1,0:T(1,128)} %bitcast.8, s32[1,256]{1,0:T(1,128)} %bitcast.9, s32[32,256]{1,0:T(8,128)} %constant.12.clone.refs_4_, bf16[1024,128]{1,0:T(8,128)(2,1)} %bitcast.5, bf16[768,32]{1,0:T(8,128)(2,1)} %constant.13.clone.refs_6_, ...), custom_call_target="tpu_custom_call" | custom-call | flops 3000000000 | bytes 2000000 | tf_op jit(solution)/shard_map/pallas_call | solution.py:448
  21.6 0.8 %copy.14 = f32[4,16,2048]{2,1,0:T(8,128)} copy(f32[4,16,2048]{2,1,0:T(8,128)S(1)} %shard_map.118) | data formatting | bytes 1048576
